TPU v7x, 32 devices: a whole 2x2x4 slice. The times are simulated.
32 devices in a mesh: grp: 2 (over x), ctx: 16 (over z, y, core).
Axes of the slice: x: 2, y: 2, z: 4, core: 2. Of those that a mesh axis runs over, the one named last changes fastest.
Arguments:
- query_proj: bfloat16 [4096, 4096], P(('grp', 'ctx')), parts along dimension 0, may hold values from -6 to 6
- key_proj: bfloat16 [4096, 4096], P(('grp', 'ctx')), parts along dimension 0, may hold values from -6 to 6
- value_proj: bfloat16 [4096, 4096], P(('grp', 'ctx')), parts along dimension 0, may hold values from -6 to 6
- out_grad: bfloat16 [4096, 4096], P(('grp', 'ctx')), parts along dimension 0, may hold values from -18 to 18
- short_taps: bfloat16 [7, 12288], replicated, may hold values from -2.5 to 2.5
- medium_taps: bfloat16 [256, 128], replicated, may hold values from -6 to 6
- doc_starts: int32 [32, 2], P(('grp', 'ctx')), parts along dimension 0, may hold values from 0 to 1023
- continues: int32 [32], P(('grp', 'ctx')), parts along dimension 0, may hold values 0 or 1
Outputs:
- gated: bfloat16 [4096, 4096], P(('grp', 'ctx')), parts along dimension 0
- grad_query: bfloat16 [4096, 4096], P(('grp', 'ctx')), parts along dimension 0
- grad_key: bfloat16 [4096, 4096], P(('grp', 'ctx')), parts along dimension 0
- grad_value: bfloat16 [4096, 4096], P(('grp', 'ctx')), parts along dimension 0
- grad_short: float32 [14, 12288], P('grp'), parts along dimension 0
- grad_medium: float32 [512, 128], P('grp'), parts along dimension 0
There are 2 independent parts, one for each index of `grp`. A program takes and returns all parts, laid end to end along the dimension named above; an argument that names none is the same for every part. Nothing has to cross between parts.
Inputs may be any that keep to these rules, and one draw needn't show every extreme that they name: `doc_starts`: an entry below 128 is the offset of a document start in that block; larger entries mark no start.
All inputs are finite; a program needn't handle non-finite values. No bound on the sum of `continues` on one device may be relied on, other than what follows from the above.
Results may differ from a plain program's by a relative error of at most 0.0059.
Values may be sent and summed in bfloat16 or wider, within the bound.
A program may use at most 192 MiB of HBM per device.

v0:
```python
import math

import jax
import jax.numpy as jnp
from jax import lax
from jax.sharding import PartitionSpec as P


def from_behind(value, axis, steps):
    count = lax.axis_size(axis)
    leading, last = (max(0, -steps), min(count, count - steps))
    return lax.ppermute(value, axis, [(source, source + steps) for source in range(leading, last)])


def padded(array, sides, width):
    for axis, dim in sides:
        peers, length = (lax.axis_size(axis), array.shape[dim])
        up = [(i, (i + 1) % peers) for i in range(peers - 1)]
        down = [(j, i) for i, j in up]
        last = lax.slice_in_dim(array, length - width, length, axis=dim)
        leading = lax.slice_in_dim(array, 0, width, axis=dim)
        before = lax.ppermute(last, axis, up)
        after = lax.ppermute(leading, axis, down)
        array = jnp.concatenate([before, array, after], axis=dim)
    return array


def block_segments(doc_starts, continues, length):
    position = jnp.arange(length, dtype=jnp.int32)
    listed = jnp.any(doc_starts[0][:, None] == position[None, :], axis=0)
    opened = listed | (position == 0) & (continues[0] == 0)
    return jnp.cumsum(opened.astype(jnp.int32))


def lag_onehot(target_count, source_count, offset, allowed):
    target = jnp.arange(target_count, dtype=jnp.int32)[:, None]
    source = jnp.arange(source_count, dtype=jnp.int32)[None, :]
    lagged = target + offset - source
    levels = jnp.arange(offset + 1, dtype=jnp.int32)[:, None, None]
    return ((lagged[None] == levels) & allowed[None]).astype(jnp.bfloat16)


def local(
    query_proj, key_proj, value_proj, out_grad, short_taps, medium_taps, doc_starts, continues
):
    length, channels = query_proj.shape
    groups, med_len = medium_taps.shape
    group_size = channels // groups
    fir_len = short_taps.shape[0]
    long_reach = med_len - 1
    short_reach = fir_len - 1
    segment = block_segments(doc_starts, continues, length)
    opening = (segment == 0).astype(jnp.float32)[:, None]
    closing = (segment == segment[length - 1]).astype(jnp.float32)[:, None]
    inputs = jnp.concatenate([query_proj, key_proj, value_proj], axis=1)
    tail_rows = (inputs[length - short_reach :] * closing[length - short_reach :]).astype(
        jnp.bfloat16
    )
    before = from_behind(tail_rows, "ctx", 1)
    inputs_ext = jnp.concatenate([before, inputs], axis=0)
    back_labels = jnp.concatenate([jnp.zeros((short_reach,), jnp.int32), segment])
    taps_f = short_taps.astype(jnp.float32)
    filtered = jnp.zeros((length, 3 * channels), jnp.float32)
    back_masks = []
    for tap_index in range(fir_len):
        first_row = short_reach - tap_index
        same_doc = (back_labels[first_row : first_row + length] == segment).astype(jnp.float32)[
            :, None
        ]
        back_masks.append(same_doc)
        filtered = (
            filtered
            + taps_f[tap_index][None, :]
            * inputs_ext[first_row : first_row + length].astype(jnp.float32)
            * same_doc
        )
    query_f = filtered[:, :channels]
    key_f = filtered[:, channels : 2 * channels]
    value_f = filtered[:, 2 * channels :]
    mixed = (key_f * value_f).astype(jnp.bfloat16)
    conv_grad = (out_grad.astype(jnp.float32) * query_f).astype(jnp.bfloat16)
    extent = length + long_reach
    ext_labels = jnp.concatenate([jnp.zeros((long_reach,), jnp.int32), segment])
    allowed_ext = ext_labels[None, :] == segment[:, None]
    lag_table = lag_onehot(length, extent, long_reach, allowed_ext)
    toeplitz = jnp.einsum(
        "gl,lte->gte", medium_taps, lag_table, preferred_element_type=jnp.float32
    ).astype(jnp.bfloat16)
    pair_table = lag_onehot(
        long_reach, long_reach, long_reach, jnp.ones((long_reach, long_reach), jnp.bool_)
    )
    couple_tile = jnp.einsum(
        "gl,lab->gab", medium_taps, pair_table, preferred_element_type=jnp.float32
    ).astype(jnp.bfloat16)
    stacked = jnp.concatenate(
        [(mixed * closing).astype(jnp.bfloat16), (conv_grad * opening).astype(jnp.bfloat16)], axis=1
    )
    rimmed = padded(stacked, (("ctx", 0),), long_reach)
    mixed_before = rimmed[:long_reach, :channels]
    grad_after = rimmed[length + long_reach :, channels:]
    mixed_ext = jnp.concatenate([mixed_before, mixed], axis=0)
    grouped_ext = mixed_ext.reshape(extent, groups, group_size)
    own_block = toeplitz[:, :, long_reach:]
    long_conv = jnp.einsum(
        "gte,egc->tgc", toeplitz, grouped_ext, preferred_element_type=jnp.float32
    ).reshape(length, channels)
    gated = (query_f * long_conv).astype(jnp.bfloat16)
    grouped_grad = conv_grad.reshape(length, groups, group_size)
    own_grad = jnp.einsum(
        "gts,tgc->sgc", own_block, grouped_grad, preferred_element_type=jnp.float32
    ).reshape(length, channels)
    edge_grad = jnp.einsum(
        "gab,agc->bgc",
        couple_tile,
        grad_after.reshape(long_reach, groups, group_size),
        preferred_element_type=jnp.float32,
    ).reshape(long_reach, channels)
    edge_grad = edge_grad * closing[length - long_reach :]
    mixed_grad = own_grad + jnp.concatenate(
        [jnp.zeros((length - long_reach, channels), jnp.float32), edge_grad], axis=0
    )
    block_rows = 16
    window = block_rows + long_reach

    def add_diagonals(block_index, totals):
        start = (block_index * block_rows).astype(jnp.int32)
        grad_rows = lax.dynamic_slice_in_dim(grouped_grad, start, block_rows, 0)
        window_rows = lax.dynamic_slice_in_dim(grouped_ext, start, window, 0)
        window_mask = lax.dynamic_slice(allowed_ext, (start, start), (block_rows, window)).astype(
            jnp.float32
        )
        products = jnp.einsum(
            "tgc,egc->gte", grad_rows, window_rows, preferred_element_type=jnp.float32
        )
        products = products * window_mask[None]
        widened = jnp.concatenate(
            [products, jnp.zeros((groups, block_rows, 1), jnp.float32)], axis=2
        )
        flattened = widened.reshape(groups, block_rows * (window + 1))
        flattened = jnp.concatenate(
            [flattened, jnp.zeros((groups, block_rows), jnp.float32)], axis=1
        )
        banded_stripes = flattened.reshape(groups, block_rows, window + 2)[:, :, :med_len]
        return totals + jnp.sum(banded_stripes, axis=1)

    diagonal_sums = lax.fori_loop(
        jnp.int32(0),
        jnp.int32(length // block_rows),
        add_diagonals,
        jnp.zeros((groups, med_len), jnp.float32),
    )
    long_local = jnp.flip(diagonal_sums, axis=1)
    short_grads = jnp.concatenate(
        [out_grad.astype(jnp.float32) * long_conv, mixed_grad * value_f, mixed_grad * key_f], axis=1
    ).astype(jnp.bfloat16)
    head_rows = (short_grads[:short_reach] * opening[:short_reach]).astype(jnp.bfloat16)
    head_after = from_behind(head_rows, "ctx", -1)
    grads_ext = jnp.concatenate([short_grads, head_after], axis=0)
    forward_labels = jnp.concatenate(
        [segment, jnp.full((short_reach,), segment[length - 1], jnp.int32)]
    )
    input_grad = jnp.zeros((length, 3 * channels), jnp.float32)
    short_local = []
    for tap_index in range(fir_len):
        same_doc = (forward_labels[tap_index : tap_index + length] == segment).astype(jnp.float32)[
            :, None
        ]
        input_grad = (
            input_grad
            + taps_f[tap_index][None, :]
            * grads_ext[tap_index : tap_index + length].astype(jnp.float32)
            * same_doc
        )
        first_row = short_reach - tap_index
        short_local.append(
            jnp.sum(
                short_grads.astype(jnp.float32)
                * inputs_ext[first_row : first_row + length].astype(jnp.float32)
                * back_masks[tap_index],
                axis=0,
            )
        )
    short_sum, long_sum = lax.psum((jnp.stack(short_local), long_local), "ctx")
    all_tokens = length * lax.axis_size("ctx")
    grad_short = short_sum / math.sqrt(all_tokens)
    grad_medium = long_sum / math.sqrt(all_tokens * group_size)
    grad_query = input_grad[:, :channels].astype(jnp.bfloat16)
    grad_key = input_grad[:, channels : 2 * channels].astype(jnp.bfloat16)
    grad_value = input_grad[:, 2 * channels :].astype(jnp.bfloat16)
    return (gated, grad_query, grad_key, grad_value, grad_short, grad_medium)


def solution(mesh):
    in_specs = (
        P(("grp", "ctx"), None),
        P(("grp", "ctx"), None),
        P(("grp", "ctx"), None),
        P(("grp", "ctx"), None),
        P(),
        P(),
        P(("grp", "ctx"), None),
        P(("grp", "ctx")),
    )
    out_specs = (
        P(("grp", "ctx"), None),
        P(("grp", "ctx"), None),
        P(("grp", "ctx"), None),
        P(("grp", "ctx"), None),
        P("grp", None),
        P("grp", None),
    )
    return jax.shard_map(local, mesh=mesh, in_specs=in_specs, out_specs=out_specs, check_vma=False)
```

profile of v0, /device:TPU:1, one launch (start us, length us, event | category | flops | bytes accessed | tf_op | source)
XLA Modules:
  0.0 420.3 jit_solution(6540753489904964846)
XLA Ops:
  14.5 4.5 %collective-permute-start = (bf16[6,12288]{1,0:T(8,128)(2,1)S(1)}, bf16[6,12288]{1,0:T(8,128)(2,1)S(1)}, u32[]{:S(2)}, u32[]{:S(2)}) collective-permute-start(bf16[6,12288]{1,0:T(8,128)(2,1)S(1)} %multiply_convert_fusion.7), channel_id=1, source_target_pairs={{0,1},{1,2},{2,3},{3,4},{4,5},{5,6},{6,7},{7,8},{8,9},{9,10},{10,1... | collective-permute-start | bytes 442376 | tf_op jit(solution)/shard_map/ppermute | solution.py:12
  21.6 7.4 %fusion.16 = f32[128,12288]{1,0:T(8,128)S(1)} fusion(bf16[128,12288]{1,0:T(8,128)(2,1)S(1)} %constant_dynamic-update-slice_fusion, bf16[6,12288]{1,0:T(8,128)(2,1)S(1)} %collective-permute-done, f32[128]{0:T(128)S(1)} %get-tuple-element.147, f32[12288]{0:T(1024)S(1)} %bitcast.75, f32[128]{0:T(128)S(1)} %get-tuple-element.148, f32[12288]{0:T(1024)S(1)} %bitcast.73, ...), kind=kLoop, calls=%fused_computation.41 | loop fusion | flops 69206016 | bytes 9931776 | tf_op jit(solution)/shard_map/add | solution.py:72
  29.1 2.4 multiply_convert_fusion.3
  31.6 2.3 pad_maximum_fusion.3
  33.9 1.9 collective-permute-start.2
  35.8 4.6 %collective-permute-start.1 = (bf16[127,8192]{1,0:T(8,128)(2,1)}, bf16[127,8192]{1,0:T(8,128)(2,1)}, u32[]{:S(2)}, u32[]{:S(2)}) collective-permute-start(bf16[127,8192]{1,0:T(8,128)(2,1)} %get-tuple-element.133), channel_id=1, source_target_pairs={{0,1},{1,2},{2,3},{3,4},{4,5},{5,6},{6,7},{7,8},{8,9},{9,10},{10,1... | collective-permute-start | bytes 6242312 | tf_op jit(solution)/shard_map/ppermute | solution.py:22
  42.6 25.8 %convert_bitcast_fusion = bf16[256,128,255]{0,1,2:T(8,128)(2,1)} fusion(s32[128,255]{0,1:T(8,128)S(1)} %iota_subtract_fusion, pred[128,255]{0,1:T(8,128)(4,1)S(1)} %copy.102, bf16[256,128]{1,0:T(8,128)(2,1)S(1)} %copy-done), kind=kOutput, calls=%fused_computation.15 | convolution fusion | flops 2155806720 | bytes 16940416 | tf_op jit(solution)/shard_map/gl,lte->gte/dot_general | solution.py:86
  68.3 7.7 %slice.243 = bf16[256,128,128]{0,1,2:T(8,128)(2,1)} slice(bf16[256,128,255]{0,1,2:T(8,128)(2,1)} %convert_bitcast_fusion), slice={[0:256], [0:128], [127:255]} | slice | bytes 16777216 | tf_op jit(solution)/shard_map/slice | solution.py:103
  76.0 25.8 %copy.103 = bf16[256,128,255]{2,1,0:T(8,128)(2,1)} copy(bf16[256,128,255]{0,1,2:T(8,128)(2,1)} %convert_bitcast_fusion) | data formatting | bytes 33423360 | tf_op jit(solution)/shard_map/convert_element_type | solution.py:88
  101.9 6.6 %convert_bitcast_fusion.1 = bf16[256,127,127]{0,2,1:T(8,128)(2,1)} fusion(s32[127,127]{1,0:T(8,128)S(1)} %iota_subtract_fusion.1, bf16[256,128]{1,0:T(8,128)(2,1)S(1)} %copy-done), kind=kOutput, calls=%fused_computation.21 | convolution fusion | flops 1063223680 | bytes 8388100 | tf_op jit(solution)/shard_map/gl,lab->gab/dot_general | solution.py:92
  108.6 12.4 %copy.109 = bf16[256,127,127]{2,1,0:T(8,128)(2,1)} copy(bf16[256,127,127]{0,2,1:T(8,128)(2,1)} %convert_bitcast_fusion.1) | data formatting | bytes 16516096 | tf_op jit(solution)/shard_map/convert_element_type | solution.py:94
  120.9 13.5 %copy.107 = bf16[256,128,128]{2,1,0:T(8,128)(2,1)} copy(bf16[256,128,128]{0,1,2:T(8,128)(2,1)} %slice.243) | data formatting | bytes 16777216 | tf_op jit(solution)/shard_map/slice | solution.py:103
  135.1 4.7 %fusion.58 = f32[256,16,128]{2,1,0:T(8,128)S(1)} fusion(bf16[128,256,16]{0,2,1:T(8,128)(2,1)S(1)} %bitcast.57, bf16[256,128,128]{2,1,0:T(8,128)(2,1)} %copy.107), kind=kOutput, calls=%fused_computation.132 | convolution fusion | flops 134217728 | bytes 11534336 | tf_op jit(solution)/shard_map/gts,tgc->sgc/dot_general | solution.py:109
  139.8 1.8 copy.111
  147.1 2.5 copy.101
  149.6 119.0 %while.11 = (s32[]{:T(128)}, f32[256,128]{0,1:T(8,128)}, bf16[128,256,16]{0,2,1:T(8,128)(2,1)S(1)}, bf16[255,256,16]{0,2,1:T(8,128)(2,1)}, pred[128,255]{1,0:T(8...) while((s32[]{:T(128)}, f32[256,128]{0,1:T(8,128)}, ...), condition=%wide.region_12.13_spmd.clone, body=%wide.region_10.12_spmd.clone.sunk | while | flops 19888376 | bytes 26997068 | solution.py:146
  150.4 5.3 %convolution_multiply_fusion.2 = f32[256,16,143]{2,1,0:T(8,128)} fusion(f32[16,143]{1,0:T(8,128)S(1)} %dynamic-slice_convert_fusion.2, bf16[255,256,16]{0,2,1:T(8,128)(2,1)} %get-tuple-element.210, s32[]{:T(128)S(6)} %select_n.13, bf16[128,256,16]{0,2,1:T(8,128)(2,1)S(1)} %get-tuple-element.209, s32[]{:T(128)S(6)} %select_n.12), kind=kOutput, calls=%fused_computation.clone.1 | convolution fusion | flops 19329024 | bytes 5489608 | tf_op jit(solution)/shard_map/while/body/tgc,egc->gte/dot_general | solution.py:132
  155.6 3.6 copy.117
  159.6 1.7 reshape.182
  161.3 1.7 slice_reduce_fusion.2
  164.5 5.3 %convolution_multiply_fusion.2 = f32[256,16,143]{2,1,0:T(8,128)} fusion(f32[16,143]{1,0:T(8,128)S(1)} %dynamic-slice_convert_fusion.2, bf16[255,256,16]{0,2,1:T(8,128)(2,1)} %get-tuple-element.210, s32[]{:T(128)S(6)} %select_n.13, bf16[128,256,16]{0,2,1:T(8,128)(2,1)S(1)} %get-tuple-element.209, s32[]{:T(128)S(6)} %select_n.12), kind=kOutput, calls=%fused_computation.clone.1 | convolution fusion | flops 19329024 | bytes 5489608 | tf_op jit(solution)/shard_map/while/body/tgc,egc->gte/dot_general | solution.py:132
  169.7 3.6 copy.117
  173.7 1.7 reshape.182
  175.4 1.7 slice_reduce_fusion.2
  177.1 1.6 select_add_fusion.2
  179.4 5.3 %convolution_multiply_fusion.2 = f32[256,16,143]{2,1,0:T(8,128)} fusion(f32[16,143]{1,0:T(8,128)S(1)} %dynamic-slice_convert_fusion.2, bf16[255,256,16]{0,2,1:T(8,128)(2,1)} %get-tuple-element.210, s32[]{:T(128)S(6)} %select_n.13, bf16[128,256,16]{0,2,1:T(8,128)(2,1)S(1)} %get-tuple-element.209, s32[]{:T(128)S(6)} %select_n.12), kind=kOutput, calls=%fused_computation.clone.1 | convolution fusion | flops 19329024 | bytes 5489608 | tf_op jit(solution)/shard_map/while/body/tgc,egc->gte/dot_general | solution.py:132
  184.7 3.6 copy.117
  188.7 1.7 reshape.182
  190.3 1.7 slice_reduce_fusion.2
  194.4 5.3 %convolution_multiply_fusion.2 = f32[256,16,143]{2,1,0:T(8,128)} fusion(f32[16,143]{1,0:T(8,128)S(1)} %dynamic-slice_convert_fusion.2, bf16[255,256,16]{0,2,1:T(8,128)(2,1)} %get-tuple-element.210, s32[]{:T(128)S(6)} %select_n.13, bf16[128,256,16]{0,2,1:T(8,128)(2,1)S(1)} %get-tuple-element.209, s32[]{:T(128)S(6)} %select_n.12), kind=kOutput, calls=%fused_computation.clone.1 | convolution fusion | flops 19329024 | bytes 5489608 | tf_op jit(solution)/shard_map/while/body/tgc,egc->gte/dot_general | solution.py:132
  199.7 3.6 copy.117
  203.6 1.7 reshape.182
  205.3 1.7 slice_reduce_fusion.2
  209.4 5.3 %convolution_multiply_fusion.2 = f32[256,16,143]{2,1,0:T(8,128)} fusion(f32[16,143]{1,0:T(8,128)S(1)} %dynamic-slice_convert_fusion.2, bf16[255,256,16]{0,2,1:T(8,128)(2,1)} %get-tuple-element.210, s32[]{:T(128)S(6)} %select_n.13, bf16[128,256,16]{0,2,1:T(8,128)(2,1)S(1)} %get-tuple-element.209, s32[]{:T(128)S(6)} %select_n.12), kind=kOutput, calls=%fused_computation.clone.1 | convolution fusion | flops 19329024 | bytes 5489608 | tf_op jit(solution)/shard_map/while/body/tgc,egc->gte/dot_general | solution.py:132
  214.7 3.6 copy.117
  218.6 1.7 reshape.182
  220.3 1.7 slice_reduce_fusion.2
  224.4 5.3 %convolution_multiply_fusion.2 = f32[256,16,143]{2,1,0:T(8,128)} fusion(f32[16,143]{1,0:T(8,128)S(1)} %dynamic-slice_convert_fusion.2, bf16[255,256,16]{0,2,1:T(8,128)(2,1)} %get-tuple-element.210, s32[]{:T(128)S(6)} %select_n.13, bf16[128,256,16]{0,2,1:T(8,128)(2,1)S(1)} %get-tuple-element.209, s32[]{:T(128)S(6)} %select_n.12), kind=kOutput, calls=%fused_computation.clone.1 | convolution fusion | flops 19329024 | bytes 5489608 | tf_op jit(solution)/shard_map/while/body/tgc,egc->gte/dot_general | solution.py:132
  229.7 3.6 copy.117
  233.6 1.7 reshape.182
  235.3 1.7 slice_reduce_fusion.2
  239.4 5.3 %convolution_multiply_fusion.2 = f32[256,16,143]{2,1,0:T(8,128)} fusion(f32[16,143]{1,0:T(8,128)S(1)} %dynamic-slice_convert_fusion.2, bf16[255,256,16]{0,2,1:T(8,128)(2,1)} %get-tuple-element.210, s32[]{:T(128)S(6)} %select_n.13, bf16[128,256,16]{0,2,1:T(8,128)(2,1)S(1)} %get-tuple-element.209, s32[]{:T(128)S(6)} %select_n.12), kind=kOutput, calls=%fused_computation.clone.1 | convolution fusion | flops 19329024 | bytes 5489608 | tf_op jit(solution)/shard_map/while/body/tgc,egc->gte/dot_general | solution.py:132
  244.6 3.6 copy.117
  248.6 1.7 reshape.182
  250.3 1.7 slice_reduce_fusion.2
  254.4 5.3 %convolution_multiply_fusion.2 = f32[256,16,143]{2,1,0:T(8,128)} fusion(f32[16,143]{1,0:T(8,128)S(1)} %dynamic-slice_convert_fusion.2, bf16[255,256,16]{0,2,1:T(8,128)(2,1)} %get-tuple-element.210, s32[]{:T(128)S(6)} %select_n.13, bf16[128,256,16]{0,2,1:T(8,128)(2,1)S(1)} %get-tuple-element.209, s32[]{:T(128)S(6)} %select_n.12), kind=kOutput, calls=%fused_computation.clone.1 | convolution fusion | flops 19329024 | bytes 5489608 | tf_op jit(solution)/shard_map/while/body/tgc,egc->gte/dot_general | solution.py:132
  259.6 3.6 copy.117
  263.6 1.7 reshape.182
  265.3 1.7 slice_reduce_fusion.2
  268.6 6.0 %fusion.59 = f32[256,16,127]{2,1,0:T(8,128)S(1)} fusion(bf16[127,256,16]{0,2,1:T(8,128)(2,1)} %bitcast.61, bf16[256,127,127]{2,1,0:T(8,128)(2,1)} %copy.109), kind=kOutput, calls=%fused_computation.133 | convolution fusion | flops 132128768 | bytes 11379200 | tf_op jit(solution)/shard_map/gab,agc->bgc/dot_general | solution.py:112
  274.6 1.9 copy.110
  276.5 10.8 %fusion.57 = f32[256,16,128]{2,1,0:T(8,128)S(1)} fusion(bf16[255,256,16]{0,2,1:T(8,128)(2,1)} %bitcast.11, bf16[256,128,255]{2,1,0:T(8,128)(2,1)} %copy.103), kind=kOutput, calls=%fused_computation.131 | convolution fusion | flops 267386880 | bytes 20897792 | tf_op jit(solution)/shard_map/gte,egc->tgc/dot_general | solution.py:104
  287.3 1.9 copy.104
  289.2 1.9 broadcast_multiply_fusion
  291.1 6.8 %multiply_convert_fusion.1 = (bf16[128,4096]{1,0:T(8,128)(2,1)S(1)}, bf16[128,4096]{1,0:T(8,128)(2,1)S(1)}, bf16[128,4096]{1,0:T(8,128)(2,1)}, bf16[128,4096]{1,0:T(8,128)(2,1)S(1)}) fusion(f32[128,12288]{1,0:T(8,128)} %copy-done.2, f32[128,4096]{1,0:T(8,128)} %copy.111, f32[127,4096]{1,0:T(8,128)S(1)} %broadcast_multiply_fusion, f32[128,4096]{1,0:T(8,128)} %copy.104, ...), kind=kLoop, calls=%fused_computation.85 | loop fusion | flops 5242880 | bytes 17809408 | tf_op jit(solution)/shard_map/convert.4
  299.3 2.0 collective-permute-start.3
  301.4 6.9 %fusion.40 = (f32[12288]{0:T(1024)S(1)}, f32[12288]{0:T(1024)}, f32[12288]{0:T(1024)}, f32[12288]{0:T(1024)}) fusion(f32[128]{0:T(128)S(1)} %get-tuple-element.148, bf16[128,12288]{1,0:T(8,128)(2,1)S(1)} %copy-done.4, bf16[6,12288]{1,0:T(8,128)(2,1)S(1)} %copy-done.8, bf16[128,4096]{1,0:T(8,128)(2,1)S(1)} %get-tuple-element.123, ...), kind=kLoop, calls=%fused_computation.65 | loop fusion | flops 47136768 | bytes 6637056 | tf_op jit(solution)/shard_map/reduce_sum | solution.py:176
  308.3 5.8 %fusion.42 = (f32[12288]{0:T(1024)}, f32[12288]{0:T(1024)}, f32[12288]{0:T(1024)}) fusion(bf16[128,12288]{1,0:T(8,128)(2,1)S(1)} %copy-done.4, bf16[6,12288]{1,0:T(8,128)(2,1)S(1)} %copy-done.8, f32[128]{0:T(128)S(1)} %get-tuple-element.147, bf16[128,4096]{1,0:T(8,128)(2,1)S(1)} %get-tuple-element.123, bf16[128,4096]{1,0:T(8,128)(2,1)S(1)} %get-tuple-element.122, ...), kind=kLoop, calls=%fused_computation.67 | loop fusion | flops 42430464 | bytes 6587904 | tf_op jit(solution)/shard_map/reduce_sum | solution.py:176
  315.1 2.0 stack.31
  317.1 3.2 pad_maximum_fusion
  320.3 9.9 %fusion.29 = bf16[128,12288]{1,0:T(8,128)(2,1)S(1)} fusion(bf16[134,12288]{1,0:T(8,128)(2,1)S(1)} %pad_maximum_fusion, f32[128]{0:T(128)S(1)} %copy-done.27, f32[128]{0:T(128)S(1)} %copy-done.26, f32[128]{0:T(128)S(1)} %copy-done.23, f32[128]{0:T(128)S(1)} %copy-done.24, f32[128]{0:T(128)S(1)} %copy-done.25, f32[128]{0:T(128)S(1)} %copy-done.22, ...), kind=kLoop, calls=%fused_computation.54 | loop fusion | flops 50331648 | bytes 25512960 | tf_op jit(solution)/shard_map/convert.2
  330.2 1.7 fusion.55
  331.9 78.2 %all-reduce.9.cloned.1.call-done = (f32[7,12288]{1,0:T(8,128)}, f32[256,128]{1,0:T(8,128)}) async-done(((f32[7,12288]{1,0:T(8,128)}, f32[256,128]{1,0:T(8,128)}), (f32[7,12288]{1,0:T(8,128)}, f32[256,128]{1,0:T(8,128)})) %all-reduce.9.cloned.1.call-update) | async-done | bytes 475152 | tf_op jit(solution)/shard_map/psum | solution.py:183
  410.1 1.8 broadcast_multiply_fusion.1
  (128 shorter events, 40.3 us)
Async XLA Ops:
  7.2 35.4 %copy-start = (bf16[256,128]{1,0:T(8,128)(2,1)S(1)}, bf16[256,128]{1,0:T(8,128)(2,1)}, u32[]{:S(2)}) copy-start(bf16[256,128]{1,0:T(8,128)(2,1)} %param.15) | copy-start | bytes 196612
  7.2 11.9 %copy-start.9 = (bf16[7,12288]{1,0:T(8,128)(2,1)S(1)}, bf16[7,12288]{1,0:T(8,128)(2,1)}, u32[]{:S(2)}) copy-start(bf16[7,12288]{1,0:T(8,128)(2,1)} %param.14) | copy-start | bytes 516100
  7.2 402.9 %all-reduce.9.cloned.1.call-start = ((), (), s32[]{:S(2)}) async-start(), calls=%async_computation | async-start | bytes 1048576 | tf_op jit(solution)/shard_map/psum | solution.py:183
  13.0 16.1 %copy-start.6 = (bf16[128,4096]{1,0:T(8,128)(2,1)S(1)}, bf16[128,4096]{1,0:T(8,128)(2,1)}, u32[]{:S(2)}) copy-start(bf16[128,4096]{1,0:T(8,128)(2,1)} %param.13) | copy-start | bytes 3145732
  14.4 7.3 %copy-start.3 = (bf16[128,12288]{1,0:T(8,128)(2,1)}, bf16[128,12288]{1,0:T(8,128)(2,1)S(1)}, u32[]{:S(2)}) copy-start(bf16[128,12288]{1,0:T(8,128)(2,1)S(1)} %constant_dynamic-update-slice_fusion) | copy-start | bytes 9437188
  14.5 7.1 %collective-permute-start = (bf16[6,12288]{1,0:T(8,128)(2,1)S(1)}, bf16[6,12288]{1,0:T(8,128)(2,1)S(1)}, u32[]{:S(2)}, u32[]{:S(2)}) collective-permute-start(bf16[6,12288]{1,0:T(8,128)(2,1)S(1)} %multiply_convert_fusion.7), channel_id=1, source_target_pairs={{0,1},{1,2},{2,3},{3,4},{4,5},{5,6},{6,7},{7,8},{8,9},{9,10},{10,1... | collective-permute-start | bytes 442376 | tf_op jit(solution)/shard_map/ppermute | solution.py:12
  19.4 9.6 %copy-start.10 = (f32[1,12288]{1,0:T(1,128)}, f32[1,12288]{1,0:T(1,128)S(1)}, u32[]{:S(2)}) copy-start(f32[1,12288]{1,0:T(1,128)S(1)} %get-tuple-element.135) | copy-start | bytes 147460
  19.4 9.6 %copy-start.11 = (f32[1,12288]{1,0:T(1,128)}, f32[1,12288]{1,0:T(1,128)S(1)}, u32[]{:S(2)}) copy-start(f32[1,12288]{1,0:T(1,128)S(1)} %get-tuple-element.136) | copy-start | bytes 147460
  19.4 9.6 %copy-start.12 = (f32[1,12288]{1,0:T(1,128)}, f32[1,12288]{1,0:T(1,128)S(1)}, u32[]{:S(2)}) copy-start(f32[1,12288]{1,0:T(1,128)S(1)} %get-tuple-element.137) | copy-start | bytes 147460
  19.4 9.6 %copy-start.13 = (f32[1,12288]{1,0:T(1,128)}, f32[1,12288]{1,0:T(1,128)S(1)}, u32[]{:S(2)}) copy-start(f32[1,12288]{1,0:T(1,128)S(1)} %get-tuple-element.138) | copy-start | bytes 147460
  19.4 9.6 %copy-start.14 = (f32[1,12288]{1,0:T(1,128)}, f32[1,12288]{1,0:T(1,128)S(1)}, u32[]{:S(2)}) copy-start(f32[1,12288]{1,0:T(1,128)S(1)} %get-tuple-element.139) | copy-start | bytes 147460
  19.4 9.6 %copy-start.15 = (f32[1,12288]{1,0:T(1,128)}, f32[1,12288]{1,0:T(1,128)S(1)}, u32[]{:S(2)}) copy-start(f32[1,12288]{1,0:T(1,128)S(1)} %get-tuple-element.140) | copy-start | bytes 147460
  20.8 8.3 %copy-start.16 = (f32[128]{0:T(128)}, f32[128]{0:T(128)S(1)}, u32[]{:S(2)}) copy-start(f32[128]{0:T(128)S(1)} %get-tuple-element.149) | copy-start | bytes 1540
  20.8 8.3 %copy-start.18 = (f32[128]{0:T(128)}, f32[128]{0:T(128)S(1)}, u32[]{:S(2)}) copy-start(f32[128]{0:T(128)S(1)} %get-tuple-element.150) | copy-start | bytes 1540
  20.8 10.8 %copy-start.20 = (f32[128]{0:T(128)}, f32[128]{0:T(128)S(1)}, u32[]{:S(2)}) copy-start(f32[128]{0:T(128)S(1)} %get-tuple-element.146) | copy-start | bytes 1540
  21.6 7.5 %copy-start.7 = (bf16[6,12288]{1,0:T(8,128)(2,1)}, bf16[6,12288]{1,0:T(8,128)(2,1)S(1)}, u32[]{:S(2)}) copy-start(bf16[6,12288]{1,0:T(8,128)(2,1)S(1)} %collective-permute-done) | copy-start | bytes 442372
  29.1 4.8 %copy-start.2 = (f32[128,12288]{1,0:T(8,128)}, f32[128,12288]{1,0:T(8,128)S(1)}, u32[]{:S(2)}) copy-start(f32[128,12288]{1,0:T(8,128)S(1)} %fusion.16) | copy-start | bytes 18874372
  33.9 107.7 %collective-permute-start.2 = (bf16[127,8192]{1,0:T(8,128)(2,1)}, bf16[127,8192]{1,0:T(8,128)(2,1)}, u32[]{:S(2)}, u32[]{:S(2)}) collective-permute-start(bf16[127,8192]{1,0:T(8,128)(2,1)} %get-tuple-element.132), channel_id=1, source_target_pairs={{1,0},{2,1},{3,2},{4,3},{5,4},{6,5},{7,6},{8,7},{9,8},{10,9},{11,1... | collective-permute-start | bytes 6242312 | tf_op jit(solution)/shard_map/ppermute | solution.py:23
  35.8 108.5 %collective-permute-start.1 = (bf16[127,8192]{1,0:T(8,128)(2,1)}, bf16[127,8192]{1,0:T(8,128)(2,1)}, u32[]{:S(2)}, u32[]{:S(2)}) collective-permute-start(bf16[127,8192]{1,0:T(8,128)(2,1)} %get-tuple-element.133), channel_id=1, source_target_pairs={{0,1},{1,2},{2,3},{3,4},{4,5},{5,6},{6,7},{7,8},{8,9},{9,10},{10,1... | collective-permute-start | bytes 6242312 | tf_op jit(solution)/shard_map/ppermute | solution.py:22
  276.5 12.7 %copy-start.28 = (f32[127]{0:T(128)S(1)}, f32[127]{0:T(128)}, u32[]{:S(2)}) copy-start(f32[127]{0:T(128)} %slice.198) | copy-start | bytes 1528
  297.9 0.7 copy-start.21
  297.9 3.5 copy-start.4
  297.9 3.5 copy-start.8
  297.9 3.5 copy-start.17
  297.9 3.5 copy-start.19
  299.3 14.8 %copy-start.5 = (f32[256,128]{0,1:T(8,128)S(1)}, f32[256,128]{0,1:T(8,128)}, u32[]{:S(2)}) copy-start(f32[256,128]{0,1:T(8,128)} %get-tuple-element.33) | copy-start | bytes 393220
  299.3 17.8 %collective-permute-start.3 = (bf16[6,12288]{1,0:T(8,128)(2,1)}, bf16[6,12288]{1,0:T(8,128)(2,1)}, u32[]{:S(2)}, u32[]{:S(2)}) collective-permute-start(bf16[6,12288]{1,0:T(8,128)(2,1)} %multiply_convert_fusion.6), channel_id=1, source_target_pairs={{1,0},{2,1},{3,2},{4,3},{5,4},{6,5},{7,6},{8,7},{9,8},{10,9},{11,1... | collective-permute-start | bytes 442376 | tf_op jit(solution)/shard_map/ppermute | solution.py:12
  308.3 12.0 %copy-start.22 = (f32[128]{0:T(128)S(1)}, f32[128]{0:T(128)}, u32[]{:S(2)}) copy-start(f32[128]{0:T(128)} %get-tuple-element.141) | copy-start | bytes 1540
  308.3 12.0 %copy-start.23 = (f32[128]{0:T(128)S(1)}, f32[128]{0:T(128)}, u32[]{:S(2)}) copy-start(f32[128]{0:T(128)} %get-tuple-element.142) | copy-start | bytes 1540
  308.3 12.0 %copy-start.24 = (f32[128]{0:T(128)S(1)}, f32[128]{0:T(128)}, u32[]{:S(2)}) copy-start(f32[128]{0:T(128)} %get-tuple-element.143) | copy-start | bytes 1540
  308.3 12.0 %copy-start.25 = (f32[128]{0:T(128)S(1)}, f32[128]{0:T(128)}, u32[]{:S(2)}) copy-start(f32[128]{0:T(128)} %get-tuple-element.144) | copy-start | bytes 1540
  308.3 12.0 %copy-start.26 = (f32[128]{0:T(128)S(1)}, f32[128]{0:T(128)}, u32[]{:S(2)}) copy-start(f32[128]{0:T(128)} %get-tuple-element.145) | copy-start | bytes 1540
  314.1 6.2 %copy-start.27 = (f32[128]{0:T(128)S(1)}, f32[128]{0:T(128)}, u32[]{:S(2)}) copy-start(f32[128]{0:T(128)} %get-tuple-element.153) | copy-start | bytes 1540
  320.3 93.2 %copy-start.1 = (bf16[256,128]{1,0:T(8,128)(2,1)S(1)}, bf16[256,128]{1,0:T(8,128)(2,1)}, u32[]{:S(2)}) copy-start(bf16[256,128]{1,0:T(8,128)(2,1)} %param.15) | copy-start | bytes 196612
Sparse Core Ops, SparseCore 0:
  317.2 92.8 all-reduce.8
where the time goes:
time: 424 us; the launch traced here: 420 us
  local copies, waits for them, and re-layouts  129 us (30%)
  matrix products  96 us (23%)
  other arithmetic  88.2 us (21%)
  waiting for transfers between devices  79.1 us (19%)
  between operations  15.3 us (4%)
  starting transfers between devices  13.1 us (3%)
    psum x1, waiting for transfers between devices, local(): short_sum, long_sum = lax.psum((jnp.stack(short_local), long_local), 'ctx')  78.2 us
    dot_general x8, matrix products, add_diagonals(): jnp.einsum('tgc,egc->gte', grad_rows, window_rows, preferred_element_type...  42.1 us
    while x8, local copies, waits for them, and re-layouts  28.9 us
    convert_element_type x1, local copies, waits for them, and re-layouts, local(): toeplitz = jnp.einsum('gl,lte->gte', medium_taps, lag_table, preferred_el...  25.8 us
    dot_general x1, matrix products, local(): jnp.einsum('gl,lte->gte', medium_taps, lag_table, preferred_element_type=...  25.8 us
    slice x2, local copies, waits for them, and re-layouts, local(): own_block = toeplitz[:, :, long_reach:]  21.2 us
    another operation x2, other arithmetic  16.6 us
    reduce_sum x8, other arithmetic, add_diagonals(): return totals + jnp.sum(banded_stripes, axis=1)  13.9 us
  transfers between devices with their start and end apart: 5, of which 2 were waited for; matrix products, arithmetic and copies ran while one was open for 32% of the time, Pallas kernels for 0%

commit v1 on v0

v1 whole, which is shorter than its diff:
```python
import functools
import math

import jax
import jax.numpy as jnp
from jax import lax
from jax.experimental import pallas as pl
from jax.experimental.pallas import tpu as pltpu
from jax.sharding import PartitionSpec as P

LANES = 128
HALO = 8
WIDE = 512
VMEM_BYTES = 48 * 1024 * 1024
F32 = jnp.float32
BF16 = jnp.bfloat16


def labels(position, starts, flag, length):
    position = jnp.minimum(position, length - 1)
    label = (flag[0] == 0).astype(jnp.int32)
    label = label + (starts[0, 0] <= position).astype(jnp.int32)
    label = label + (starts[0, 1] <= position).astype(jnp.int32)
    return jnp.where(position < 0, 0, label)


def short_forward(
    starts, flag, q_ref, k_ref, v_ref, og_ref, hq_ref, hk_ref, hv_ref, wq_ref, wk_ref, wv_ref,
    mixed_ref, grad_ref, mixed_out_ref, grad_out_ref, qf_ref, kf_ref, vf_ref, masks, ext,
):
    length = q_ref.shape[0]
    taps = wq_ref.shape[0]
    row = lax.broadcasted_iota(jnp.int32, (length, LANES), 0)

    @pl.when(pl.program_id(0) == 0)
    def _():
        own = labels(row, starts, flag, length)
        last = labels(row * 0 + (length - 1), starts, flag, length)
        for j in range(taps):
            masks[j] = (labels(row - j, starts, flag, length) == own).astype(F32)
        masks[taps] = (own == last).astype(F32)
        masks[taps + 1] = (own == 0).astype(F32)

    def tile(i, carry):
        cols = pl.ds(pl.multiple_of(i * LANES, LANES), LANES)
        filtered = []
        for n, (x, h, w, out) in enumerate(
            ((q_ref, hq_ref, wq_ref, qf_ref), (k_ref, hk_ref, wk_ref, kf_ref), (v_ref, hv_ref, wv_ref, vf_ref))
        ):
            ext[n, :HALO, :] = h[:, cols]
            ext[n, HALO:, :] = x[:, cols].astype(F32)
            weight = w[:, cols]
            total = weight[0:1] * ext[n, HALO:, :]
            for j in range(1, taps):
                total = total + weight[j : j + 1] * (ext[n, HALO - j : HALO - j + length, :] * masks[j])
            out[:, cols] = total
            filtered.append(total)
        query, key, value = filtered
        mixed = (key * value).astype(BF16)
        mixed_ref[:, cols] = mixed
        mixed_out_ref[:, cols] = (mixed.astype(F32) * masks[taps]).astype(BF16)
        grad = (og_ref[:, cols].astype(F32) * query).astype(BF16)
        grad_ref[:, cols] = grad
        grad_out_ref[:, cols] = (grad.astype(F32) * masks[taps + 1]).astype(BF16)
        return carry

    lax.fori_loop(0, q_ref.shape[1] // LANES, tile, 0)


def long_filter(
    starts, flag, mixed_ref, before_ref, grad_ref, after_ref, qf_ref, kf_ref, vf_ref, og_ref,
    taps_ref, turned_ref, gated_ref, sq_ref, sk_ref, sv_ref, dmed_ref,
    masks, rev_masks, back, left, left_t, left_p, prod, prod_t, prod_p,
):
    length = mixed_ref.shape[0]
    size = mixed_ref.shape[1] // taps_ref.shape[0]
    per_tile = LANES // size
    row = lax.broadcasted_iota(jnp.int32, (length, length), 0)
    col = lax.broadcasted_iota(jnp.int32, (length, length), 1)

    @pl.when(pl.program_id(0) == 0)
    def _():
        label_row = labels(row, starts, flag, length)
        label_col = labels(col, starts, flag, length)
        last = labels(row * 0 + (length - 1), starts, flag, length)
        same = label_row == label_col
        masks[0] = ((col <= row) & same).astype(F32).astype(BF16)
        masks[1] = ((col > row) & (label_row == 0)).astype(F32).astype(BF16)
        masks[2] = ((col >= row) & same).astype(F32).astype(BF16)
        masks[3] = ((col < row) & (label_row == last)).astype(F32).astype(BF16)
        rev = (length - 1) - row
        label_rev = labels(rev, starts, flag, length)
        rev_masks[0] = ((col <= rev) & (label_rev == label_col)).astype(F32)
        rev_masks[1] = ((col > rev) & (label_rev == 0)).astype(F32)
        back[...] = (row + col == length - 1).astype(F32).astype(BF16)

    group_of_lane = lax.broadcasted_iota(jnp.int32, (length, LANES), 1) // size

    def tile(i, carry):
        cols = pl.ds(pl.multiple_of(i * LANES, LANES), LANES)
        rows = pl.ds(pl.multiple_of(i * per_tile, per_tile), per_tile)
        taps = taps_ref[rows, :]
        turned = turned_ref[rows, :]
        mixed = mixed_ref[:, cols]
        grad = grad_ref[:, cols]
        both = jnp.concatenate([mixed, before_ref[:, cols]], axis=0)
        both_grad = jnp.concatenate([grad, after_ref[:, cols]], axis=0)
        flipped = jnp.dot(back[...], grad, preferred_element_type=F32)
        for g in range(per_tile):
            part = slice(g * length, (g + 1) * length)
            ring = pltpu.roll(
                jnp.broadcast_to(turned[g : g + 1], (length, length)), 0, 1, stride=1, stride_axis=0
            ).astype(BF16)
            left[part, :length] = ring * masks[0]
            left[part, length:] = ring * masks[1]
            ring_t = pltpu.roll(
                jnp.broadcast_to(taps[g : g + 1], (length, length)), 0, 1, stride=1, stride_axis=0
            ).astype(BF16)
            left_t[part, :length] = ring_t * masks[2]
            left_t[part, length:] = ring_t * masks[3]
            left_p[part, :] = jnp.where(group_of_lane == g, flipped, 0.0).astype(BF16)
        prod[...] = jnp.dot(left[...], both, preferred_element_type=F32)
        prod_t[...] = jnp.dot(left_t[...], both_grad, preferred_element_type=F32)
        prod_p[...] = lax.dot_general(
            left_p[...], both, (((1,), (1,)), ((), ())), preferred_element_type=F32
        )
        conv = prod[:length, :]
        mixed_grad = prod_t[:length, :]
        sums = []
        for g in range(per_tile):
            part = slice(g * length, (g + 1) * length)
            if g:
                conv = jnp.where(group_of_lane == g, prod[part, :], conv)
                mixed_grad = jnp.where(group_of_lane == g, prod_t[part, :], mixed_grad)
            pair = prod_p[part, :length] * rev_masks[0] + prod_p[part, length:] * rev_masks[1]
            pair = pltpu.roll(pair, 0, 1, stride=1, stride_axis=0)
            sums.append(jnp.sum(pair, axis=0, keepdims=True))
        dmed_ref[rows, :] = jnp.concatenate(sums, axis=0)
        gated_ref[:, cols] = (qf_ref[:, cols] * conv).astype(BF16)
        sq_ref[:, cols] = (og_ref[:, cols].astype(F32) * conv).astype(BF16)
        sk_ref[:, cols] = (mixed_grad * vf_ref[:, cols]).astype(BF16)
        sv_ref[:, cols] = (mixed_grad * kf_ref[:, cols]).astype(BF16)
        return carry

    lax.fori_loop(0, mixed_ref.shape[1] // LANES, tile, 0)


def short_backward(
    starts, flag, sq_ref, sk_ref, sv_ref, hq_ref, hk_ref, hv_ref, q_ref, k_ref, v_ref, wq_ref, wk_ref, wv_ref,
    gq_ref, gk_ref, gv_ref, dq_ref, dk_ref, dv_ref, masks, ext,
):
    length = q_ref.shape[0]
    taps = wq_ref.shape[0]
    row = lax.broadcasted_iota(jnp.int32, (length, LANES), 0)

    @pl.when(pl.program_id(0) == 0)
    def _():
        own = labels(row, starts, flag, length)
        for j in range(taps):
            masks[j] = (labels(row + j, starts, flag, length) == own).astype(F32)

    def tile(i, carry):
        cols = pl.ds(pl.multiple_of(i * LANES, LANES), LANES)
        for n, (s, h, x, w, out, d) in enumerate((
            (sq_ref, hq_ref, q_ref, wq_ref, gq_ref, dq_ref),
            (sk_ref, hk_ref, k_ref, wk_ref, gk_ref, dk_ref),
            (sv_ref, hv_ref, v_ref, wv_ref, gv_ref, dv_ref),
        )):
            ext[n, :length, :] = s[:, cols].astype(F32)
            ext[n, length:, :] = h[:, cols]
            weight = w[:, cols]
            signal = x[:, cols].astype(F32)
            total = jnp.zeros((length, LANES), F32)
            sums = []
            for j in range(taps):
                moved = ext[n, j : j + length, :]
                if j:
                    moved = moved * masks[j]
                total = total + weight[j : j + 1] * moved
                sums.append(jnp.sum(signal * moved, axis=0, keepdims=True))
            sums.append(jnp.zeros((HALO - taps, LANES), F32))
            out[:, cols] = total.astype(BF16)
            d[:, cols] = jnp.concatenate(sums, axis=0)
        return carry

    lax.fori_loop(0, q_ref.shape[1] // LANES, tile, 0)


def all_sum(count, short_scale, med_scale, short_ref, med_ref, short_out, med_out, short_in, med_in, send, recv):
    me = lax.axis_index("ctx")
    columns = short_ref.shape[1] // count
    rows = med_ref.shape[0] // count

    def cols_of(peer):
        return pl.ds(pl.multiple_of(peer * columns, columns), columns)

    def rows_of(peer):
        return pl.ds(pl.multiple_of(peer * rows, rows), rows)

    barrier = pltpu.get_barrier_semaphore()
    for d in range(1, count):
        pl.semaphore_signal(
            barrier, inc=1, device_id={"ctx": lax.rem(me + d, count)}, device_id_type=pl.DeviceIdType.MESH
        )
    pl.semaphore_wait(barrier, count - 1)

    def copy(src, dst, phase, d):
        return pltpu.make_async_remote_copy(
            src_ref=src, dst_ref=dst, send_sem=send.at[phase, d], recv_sem=recv.at[phase, d],
            device_id={"ctx": lax.rem(me + d, count)}, device_id_type=pl.DeviceIdType.MESH,
        )

    first = []
    for d in range(1, count):
        peer = lax.rem(me + d, count)
        first.append(copy(short_ref.at[:, cols_of(peer)], short_in.at[d], 0, d))
        first.append(copy(med_ref.at[rows_of(peer), :], med_in.at[d], 1, d))
    for c in first:
        c.start()
    short_total = short_ref[:, cols_of(me)]
    med_total = med_ref[rows_of(me), :]
    for c in first:
        c.wait_recv()
    for d in range(1, count):
        short_total = short_total + short_in[d]
        med_total = med_total + med_in[d]
    short_out[:, cols_of(me)] = short_total * short_scale
    med_out[rows_of(me), :] = med_total * med_scale
    second = []
    for d in range(1, count):
        mine = short_out.at[:, cols_of(me)]
        second.append(copy(mine, mine, 2, d))
        mine = med_out.at[rows_of(me), :]
        second.append(copy(mine, mine, 3, d))
    for c in second:
        c.start()
    for c in second:
        c.wait_recv()
    for c in first + second:
        c.wait_send()


def params(**kwargs):
    return pltpu.CompilerParams(vmem_limit_bytes=VMEM_BYTES, **kwargs)


def local(query_proj, key_proj, value_proj, out_grad, short_taps, medium_taps, doc_starts, continues):
    length, channels = query_proj.shape
    groups, med_len = medium_taps.shape
    size = channels // groups
    fir_len = short_taps.shape[0]
    reach = fir_len - 1
    peers = lax.axis_size("ctx")
    up = [(i, i + 1) for i in range(peers - 1)]
    down = [(i + 1, i) for i in range(peers - 1)]

    position = jnp.arange(length, dtype=jnp.int32)
    segment = labels(position, doc_starts, continues, length)
    closing = (segment == segment[length - 1]).astype(F32)[:, None]
    opening = (segment == 0).astype(F32)[:, None]

    tails = jnp.concatenate([x[length - reach :] for x in (query_proj, key_proj, value_proj)], axis=1)
    tails = (tails.astype(F32) * closing[length - reach :]).astype(BF16)
    before = jnp.pad(lax.ppermute(tails, "ctx", up).astype(F32), ((HALO - reach, 0), (0, 0)))
    taps_f = short_taps.astype(F32)
    steps = channels // WIDE
    smem = [pl.BlockSpec(memory_space=pltpu.SMEM)] * 2

    def wide(rows, part=0):
        return pl.BlockSpec((rows, WIDE), lambda i: (0, i + part * steps))

    shape = jax.ShapeDtypeStruct
    half = shape((length, channels), BF16)
    full = shape((length, channels), F32)
    parts = [0, 1, 2]
    mixed, grad, mixed_out, grad_out, qf, kf, vf = pl.pallas_call(
        short_forward,
        grid=(steps,),
        in_specs=smem + [wide(length)] * 4 + [wide(HALO, p) for p in parts] + [wide(fir_len, p) for p in parts],
        out_specs=[wide(length)] * 7,
        out_shape=[half] * 4 + [full] * 3,
        scratch_shapes=[
            pltpu.VMEM((fir_len + 2, length, LANES), F32),
            pltpu.VMEM((3, HALO + length, LANES), F32),
        ],
        compiler_params=params(),
    )(doc_starts, continues, query_proj, key_proj, value_proj, out_grad, before, before, before, taps_f, taps_f, taps_f)

    mixed_before = lax.ppermute(mixed_out, "ctx", up)
    grad_after = lax.ppermute(grad_out, "ctx", down)

    med_f = medium_taps.astype(F32)
    turned = jnp.roll(jnp.flip(med_f, axis=1), 1, axis=1)
    per_tile = LANES // size
    med_spec = pl.BlockSpec((WIDE // size, med_len), lambda i: (i, 0))
    gated, sq, sk, sv, dmed = pl.pallas_call(
        long_filter,
        grid=(steps,),
        in_specs=smem + [wide(length)] * 8 + [med_spec] * 2,
        out_specs=[wide(length)] * 4 + [med_spec],
        out_shape=[half] * 4 + [shape((groups, med_len), F32)],
        scratch_shapes=[
            pltpu.VMEM((4, length, length), BF16),
            pltpu.VMEM((2, length, length), F32),
            pltpu.VMEM((length, length), BF16),
            pltpu.VMEM((per_tile * length, 2 * length), BF16),
            pltpu.VMEM((per_tile * length, 2 * length), BF16),
            pltpu.VMEM((per_tile * length, LANES), BF16),
            pltpu.VMEM((per_tile * length, LANES), F32),
            pltpu.VMEM((per_tile * length, LANES), F32),
            pltpu.VMEM((per_tile * length, 2 * length), F32),
        ],
        compiler_params=params(),
    )(doc_starts, continues, mixed, mixed_before, grad, grad_after, qf, kf, vf, out_grad, med_f, turned)

    heads = jnp.concatenate([s[:reach] for s in (sq, sk, sv)], axis=1)
    heads = (heads.astype(F32) * opening[:reach]).astype(BF16)
    after = jnp.pad(lax.ppermute(heads, "ctx", down).astype(F32), ((0, HALO - reach), (0, 0)))
    eight = shape((HALO, channels), F32)
    gq, gk, gv, dq, dk, dv = pl.pallas_call(
        short_backward,
        grid=(steps,),
        in_specs=smem
        + [wide(length)] * 3
        + [wide(HALO, p) for p in parts]
        + [wide(length)] * 3
        + [wide(fir_len, p) for p in parts],
        out_specs=[wide(length)] * 3 + [wide(HALO)] * 3,
        out_shape=[half] * 3 + [eight] * 3,
        scratch_shapes=[
            pltpu.VMEM((fir_len, length, LANES), F32),
            pltpu.VMEM((3, length + HALO, LANES), F32),
        ],
        compiler_params=params(),
    )(doc_starts, continues, sq, sk, sv, after, after, after, query_proj, key_proj, value_proj, taps_f, taps_f, taps_f)

    dshort = jnp.concatenate([dq, dk, dv], axis=1)
    tokens = length * peers
    short_scale = 1.0 / math.sqrt(tokens)
    med_scale = 1.0 / math.sqrt(tokens * size)
    if (3 * channels) % (peers * LANES) == 0 and groups % (peers * 8) == 0:
        columns, rows = 3 * channels // peers, groups // peers
        dshort, dmed = pl.pallas_call(
            functools.partial(all_sum, peers, short_scale, med_scale),
            in_specs=[pl.BlockSpec(memory_space=pltpu.VMEM)] * 2,
            out_specs=[pl.BlockSpec(memory_space=pltpu.VMEM)] * 2,
            out_shape=[shape(dshort.shape, F32), shape(dmed.shape, F32)],
            scratch_shapes=[
                pltpu.VMEM((peers, HALO, columns), F32),
                pltpu.VMEM((peers, rows, med_len), F32),
                pltpu.SemaphoreType.DMA((4, peers)),
                pltpu.SemaphoreType.DMA((4, peers)),
            ],
            compiler_params=params(collective_id=0, has_side_effects=True),
        )(dshort, dmed)
    else:
        dshort, dmed = lax.psum((dshort, dmed), "ctx")
        dshort, dmed = dshort * short_scale, dmed * med_scale
    return gated, gq, gk, gv, dshort[:fir_len], jnp.flip(dmed, axis=1)


def solution(mesh):
    tokens = P(("grp", "ctx"), None)
    in_specs = (tokens,) * 4 + (P(), P(), tokens, P(("grp", "ctx")))
    out_specs = (tokens,) * 4 + (P("grp", None), P("grp", None))
    return jax.shard_map(local, mesh=mesh, in_specs=in_specs, out_specs=out_specs, check_vma=False)
```

time: 424 us -> 136 us (0.32)
  the two profiles are of different devices: /device:TPU:1 before, /device:TPU:29 now
where the time goes in v1:
time: 136 us; the launch traced here: 135 us
  Pallas kernels  84.4 us (62%)
  starting transfers between devices  30 us (22%)
  local copies, waits for them, and re-layouts  11.6 us (9%)
  other arithmetic  5.01 us (4%)
  waiting for transfers between devices  2.3 us (2%)
  between operations  1.54 us (1%)
    pallas_call x1, Pallas kernels, local(): pl.pallas_call(functools.partial(all_sum, peers, short_scale, med_scale),...  33.7 us
    pallas_call x1, Pallas kernels, local(): pl.pallas_call(long_filter, grid=(steps,), in_specs=smem + [wide(length)]...  26.8 us
    ppermute x1, starting transfers between devices, local(): lax.ppermute(heads, 'ctx', down).astype(F32)  19.7 us
    pallas_call x1, Pallas kernels, local(): pl.pallas_call(short_backward, grid=(steps,), in_specs=smem + [wide(lengt...  12.9 us
    pallas_call x1, Pallas kernels, local(): pl.pallas_call(short_forward, grid=(steps,), in_specs=smem + [wide(length...  10.9 us
    ppermute x1, starting transfers between devices, local(): grad_after = lax.ppermute(grad_out, 'ctx', down)  7.7 us
    unnamed x13, local copies, waits for them, and re-layouts  3.28 us
    slice x3, local copies, waits for them, and re-layouts, local(): turned = jnp.roll(jnp.flip(med_f, axis=1), 1, axis=1)  3.04 us
  transfers between devices with their start and end apart: 4, of which 2 were waited for; matrix products, arithmetic and copies ran while one was open for 4% of the time, Pallas kernels for 0%

profile of v1, /device:TPU:29, one launch (start us, length us, event | category | flops | bytes accessed | tf_op | source)
XLA Modules:
  0.0 134.9 jit_solution(10611888350518249319)
XLA Ops:
  0.6 0.0 copy-start
  1.4 1.3 fusion.3
  2.7 1.3 broadcast_compare_fusion
  4.0 0.6 slice.61
  4.6 0.6 broadcast_compare_fusion.1
  5.2 0.1 slice_convert_fusion.1
  5.3 0.9 slice.56
  6.2 0.9 slice.57
  7.0 0.9 slice.58
  7.9 0.1 multiply_convert_fusion.1
  8.0 1.3 collective-permute-start
  9.3 1.0 convert_element_type.44.wq_ref.wk_ref.wv_ref
  10.3 1.3 collective-permute-done
  11.5 0.1 pad_convert_fusion.1.hq_ref.hk_ref.hv_ref
  11.6 0.0 copy-done
  11.6 0.0 copy-start.3
  11.6 0.6 copy-done.3
  12.2 0.0 copy-start.5
  12.2 0.0 copy-start.4
  12.2 10.9 %shard_map.127 = (bf16[128,4096]{1,0:T(8,128)(2,1)S(1)}, bf16[128,4096]{1,0:T(8,128)(2,1)S(1)}, bf16[128,4096]{1,0:T(8,128)(2,1)}, bf16[128,4096]{1,0:T(8,128)(2...) custom-call(s32[1,2]{1,0:T(1,128)S(1)} %copy-done.3, s32[1]{0:T(128)S(6)} %copy.15.flag, ...), custom_call_target="tpu_custom_call" | custom-call | tf_op jit(solution)/shard_map/pallas_call | solution.py:276
  23.2 0.0 copy-start.1
  23.2 1.0 copy-done.1
  24.1 1.3 collective-permute-start.1
  25.4 7.7 %collective-permute-start.2 = (bf16[128,4096]{1,0:T(8,128)(2,1)}, bf16[128,4096]{1,0:T(8,128)(2,1)}, u32[]{:S(2)}, u32[]{:S(2)}) collective-permute-start(bf16[128,4096]{1,0:T(8,128)(2,1)} %get-tuple-element.29), channel_id=1, source_target_pairs={{1,0},{2,1},{3,2},{4,3},{5,4},{6,5},{7,6},{8,7},{9,8},{10,9},{11,1... | collective-permute-start | bytes 3145736 | tf_op jit(solution)/shard_map/ppermute | solution.py:290
  33.1 0.0 copy-done.5
  33.1 0.7 slice.73
  33.8 0.7 slice.74
  34.5 0.7 convert_element_type.45.taps_ref
  35.2 1.6 %slice.66 = f32[256,127]{1,0:T(8,128)} reverse(f32[256,127]{1,0:T(8,128)} %slice.74), dimensions={1} | reverse | bytes 260096 | tf_op jit(solution)/shard_map/jit(_roll_static)/slice | solution.py:293
  36.8 1.1 pad_maximum_fusion.1.turned_ref
  37.9 0.0 collective-permute-done.1.before_ref
  37.9 0.0 collective-permute-done.2.after_ref
  37.9 0.0 copy-done.4
  38.0 0.0 copy-start.2
  38.0 0.9 copy-done.2
  38.9 26.8 %shard_map.128 = (bf16[128,4096]{1,0:T(8,128)(2,1)}, bf16[128,4096]{1,0:T(8,128)(2,1)S(1)}, bf16[128,4096]{1,0:T(8,128)(2,1)S(1)}, bf16[128,4096]{1,0:T(8,128)(2,1)S(1)}, f32[256,128]{1,0:T(8,128)S(1)}) custom-call(s32[1,2]{1,0:T(1,128)S(1)} %copy-done.4, s32[1]{0:T(128)S(6)} %copy.15.flag, bf16[128,4096]{1,0:T(8,128)(2,1)S(1)} %get-tuple-element.26.mixed_ref, ...), custom_call_target="tpu_custom_call" | custom-call | tf_op jit(solution)/shard_map/pallas_call | solution.py:296
  65.7 0.1 multiply_convert_fusion
  65.8 19.7 %collective-permute-start.3 = (bf16[6,12288]{1,0:T(8,128)(2,1)S(1)}, bf16[6,12288]{1,0:T(8,128)(2,1)S(1)}, u32[]{:S(2)}, u32[]{:S(2)}) collective-permute-start(bf16[6,12288]{1,0:T(8,128)(2,1)S(1)} %multiply_convert_fusion), channel_id=1, source_target_pairs={{1,0},{2,1},{3,2},{4,3},{5,4},{6,5},{7,6},{8,7},{9,8},{10,9},{11,1... | collective-permute-start | bytes 442376 | tf_op jit(solution)/shard_map/ppermute | solution.py:318
  85.6 1.0 collective-permute-done.3
  86.6 12.9 %shard_map.129 = (bf16[128,4096]{1,0:T(8,128)(2,1)}, bf16[128,4096]{1,0:T(8,128)(2,1)}, bf16[128,4096]{1,0:T(8,128)(2,1)}, f32[8,4096]{1,0:T(8,128)S(1)}, f32[8,4096]{1,0:T(8,128)S(1)}, /*index=5*/f32[8,4096]{1,0:T(8,128)S(1)}) custom-call(s32[1,2]{1,0:T(1,128)S(1)} %copy-done.4, s32[1]{0:T(128)S(6)} %copy.15.flag, ...), custom_call_target="tpu_custom_call" | custom-call | tf_op jit(solution)/shard_map/pallas_call | solution.py:320
  99.6 33.7 %shard_map.130 = (f32[8,12288]{1,0:T(8,128)S(1)}, f32[256,128]{1,0:T(8,128)S(1)}) custom-call(f32[8,12288]{1,0:T(8,128)S(1)} %pad_maximum_fusion.short_ref, f32[256,128]{1,0:T(8,128)S(1)} %get-tuple-element.43.med_ref), custom_call_target="tpu_custom_call" | custom-call | tf_op jit(solution)/shard_map/pallas_call | solution.py:343
  133.4 0.8 rev.5
  134.2 0.7 copy.16
  (6 shorter events, 0.1 us)
Async XLA Ops:
  0.6 10.9 %copy-start = (bf16[128,4096]{1,0:T(8,128)(2,1)S(1)}, bf16[128,4096]{1,0:T(8,128)(2,1)}, u32[]{:S(2)}) copy-start(bf16[128,4096]{1,0:T(8,128)(2,1)} %q_ref.3) | copy-start | bytes 3145732
  8.0 3.5 %collective-permute-start = (bf16[6,12288]{1,0:T(8,128)(2,1)S(1)}, bf16[6,12288]{1,0:T(8,128)(2,1)S(1)}, u32[]{:S(2)}, u32[]{:S(2)}) collective-permute-start(bf16[6,12288]{1,0:T(8,128)(2,1)S(1)} %multiply_convert_fusion.1), channel_id=1, source_target_pairs={{0,1},{1,2},{2,3},{3,4},{4,5},{5,6},{6,7},{7,8},{8,9},{9,10},{10,1... | collective-permute-start | bytes 442376 | tf_op jit(solution)/shard_map/ppermute | solution.py:264
  11.6 0.7 copy-start.3
  12.2 20.9 %copy-start.5 = (bf16[256,128]{1,0:T(8,128)(2,1)S(1)}, bf16[256,128]{1,0:T(8,128)(2,1)}, u32[]{:S(2)}) copy-start(bf16[256,128]{1,0:T(8,128)(2,1)} %param.13) | copy-start | bytes 196612
  12.2 25.7 %copy-start.4 = (s32[1,2]{1,0:T(1,128)S(1)}, s32[1,2]{1,0:T(1,128)}, u32[]{:S(2)}) copy-start(s32[1,2]{1,0:T(1,128)} %starts.5) | copy-start | bytes 28
  23.2 1.0 copy-start.1
  24.1 13.8 %collective-permute-start.1 = (bf16[128,4096]{1,0:T(8,128)(2,1)}, bf16[128,4096]{1,0:T(8,128)(2,1)S(1)}, u32[]{:S(2)}, u32[]{:S(2)}) collective-permute-start(bf16[128,4096]{1,0:T(8,128)(2,1)} %get-tuple-element.27), channel_id=1, source_target_pairs={{0,1},{1,2},{2,3},{3,4},{4,5},{5,6},{6,7},{7,8},{8,9},{9,10},{10,1... | collective-permute-start | bytes 3145736 | tf_op jit(solution)/shard_map/ppermute | solution.py:289
  25.4 12.5 %collective-permute-start.2 = (bf16[128,4096]{1,0:T(8,128)(2,1)}, bf16[128,4096]{1,0:T(8,128)(2,1)}, u32[]{:S(2)}, u32[]{:S(2)}) collective-permute-start(bf16[128,4096]{1,0:T(8,128)(2,1)} %get-tuple-element.29), channel_id=1, source_target_pairs={{1,0},{2,1},{3,2},{4,3},{5,4},{6,5},{7,6},{8,7},{9,8},{10,9},{11,1... | collective-permute-start | bytes 3145736 | tf_op jit(solution)/shard_map/ppermute | solution.py:290
  38.0 0.9 copy-start.2
  65.8 20.8 %collective-permute-start.3 = (bf16[6,12288]{1,0:T(8,128)(2,1)S(1)}, bf16[6,12288]{1,0:T(8,128)(2,1)S(1)}, u32[]{:S(2)}, u32[]{:S(2)}) collective-permute-start(bf16[6,12288]{1,0:T(8,128)(2,1)S(1)} %multiply_convert_fusion), channel_id=1, source_target_pairs={{1,0},{2,1},{3,2},{4,3},{5,4},{6,5},{7,6},{8,7},{9,8},{10,9},{11,1... | collective-permute-start | bytes 442376 | tf_op jit(solution)/shard_map/ppermute | solution.py:318

commit v2 on v0

v2 whole, which is shorter than its diff:
```python
import functools
import math

import jax
import jax.numpy as jnp
from jax import lax
from jax.experimental import pallas as pl
from jax.experimental.pallas import tpu as pltpu
from jax.sharding import PartitionSpec as P

LANES = 128
HALO = 8
WIDE = 512
SLICE = 256
EDGE = 16
PAIR = 2
VMEM_BYTES = 52 * 1024 * 1024
MESH = pl.DeviceIdType.MESH
F32 = jnp.float32
BF16 = jnp.bfloat16


def labels(position, starts, flag, length):
    position = jnp.minimum(position, length - 1)
    label = (flag[0] == 0).astype(jnp.int32)
    label = label + (starts[0, 0] <= position).astype(jnp.int32)
    label = label + (starts[0, 1] <= position).astype(jnp.int32)
    return jnp.where(position < 0, 0, label)


def layer(
    count, summed, short_scale, med_scale,
    starts, flag, q_ref, k_ref, v_ref, og_ref, w_ref, taps_ref, turned_ref,
    gated_ref, gq_ref, gk_ref, gv_ref, sums_ref,
    qf_ref, kf_ref, vf_ref, mixed_ref, grad_ref, short_ref,
    tail_out, tail_in, mixed_out, mixed_in, grad_out, grad_in, head_out, head_in, part, slots,
    back_masks, fore_masks, masks, rev_masks, back, ext, left, left_t, left_p, prod, prod_t, prod_p,
    tail_send, tail_recv, mixed_send, mixed_recv, grad_send, grad_recv, head_send, head_recv,
    part_send, part_recv, sum_send, sum_recv,
):
    length, channels = q_ref.shape
    fir_len = w_ref.shape[0]
    size = channels // taps_ref.shape[0]
    per_tile = LANES // size
    chunks = channels // WIDE
    tiles = WIDE // LANES
    slices = WIDE // SLICE
    me = lax.axis_index("ctx")
    has_before, has_after = me > 0, me < count - 1
    before, after = jnp.maximum(me - 1, 0), jnp.minimum(me + 1, count - 1)
    signals = (q_ref, k_ref, v_ref)

    def copy(src, dst, send, recv, peer):
        return pltpu.make_async_remote_copy(
            src_ref=src, dst_ref=dst, send_sem=send, recv_sem=recv, device_id={"ctx": peer}, device_id_type=MESH
        )

    def tail_copy():
        return copy(tail_out, tail_in, tail_send, tail_recv, after)

    def mixed_copy(c):
        return copy(mixed_out.at[c], mixed_in.at[c], mixed_send.at[c], mixed_recv.at[c], after)

    def grad_copy(c):
        return copy(grad_out.at[c], grad_in.at[c], grad_send.at[c], grad_recv.at[c], before)

    def head_copy(c):
        return copy(head_out.at[c], head_in.at[c], head_send.at[c], head_recv.at[c], before)

    barrier = pltpu.get_barrier_semaphore()

    def greet(peer):
        pl.semaphore_signal(barrier, inc=1, device_id={"ctx": peer}, device_id_type=MESH)

    if summed:
        for d in range(1, count):
            greet(lax.rem(me + d, count))
    else:
        pl.when(has_before)(lambda: greet(before))
        pl.when(has_after)(lambda: greet(after))

    def label(position):
        return labels(position, starts, flag, length)

    edge_row = lax.broadcasted_iota(jnp.int32, (EDGE, channels), 0) + (length - EDGE)
    edge_mask = (label(edge_row) == label(edge_row * 0 + (length - 1))).astype(F32)
    for n, x in enumerate(signals):
        tail_out[n] = (x[length - EDGE :, :].astype(F32) * edge_mask).astype(BF16)

    if summed:
        pl.semaphore_wait(barrier, count - 1)
    else:
        pl.when(has_before)(lambda: pl.semaphore_wait(barrier, 1))
        pl.when(has_after)(lambda: pl.semaphore_wait(barrier, 1))

    @pl.when(has_after)
    def _():
        tail_copy().start()

    row = lax.broadcasted_iota(jnp.int32, (length, LANES), 0)
    col = lax.broadcasted_iota(jnp.int32, (length, LANES), 1)
    own = label(row)
    across = label(col)
    last = label(row * 0 + (length - 1))
    for j in range(fir_len):
        back_masks[j] = (label(row - j) == own).astype(F32)
        fore_masks[j] = (label(row + j) == own).astype(F32)
    back_masks[fir_len] = (own == last).astype(F32)
    back_masks[fir_len + 1] = (own == 0).astype(F32)
    masks[0] = ((col <= row) & (own == across)).astype(F32).astype(BF16)
    masks[1] = ((col > row) & (own == 0)).astype(F32).astype(BF16)
    masks[2] = ((col >= row) & (own == across)).astype(F32).astype(BF16)
    masks[3] = ((col < row) & (own == last)).astype(F32).astype(BF16)
    rev = (length - 1) - row
    rev_masks[0] = ((col <= rev) & (label(rev) == across)).astype(F32)
    rev_masks[1] = ((col > rev) & (label(rev) == 0)).astype(F32)
    back[...] = (row + col == length - 1).astype(F32).astype(BF16)
    group_of_lane = col // size

    @pl.when(me == 0)
    def _():
        tail_in[...] = jnp.zeros(tail_in.shape, BF16)
        mixed_in[...] = jnp.zeros(mixed_in.shape, BF16)

    @pl.when(me == count - 1)
    def _():
        grad_in[...] = jnp.zeros(grad_in.shape, BF16)
        head_in[...] = jnp.zeros(head_in.shape, BF16)

    @pl.when(has_before)
    def _():
        tail_copy().wait_recv()

    def lanes(start):
        return pl.ds(pl.multiple_of(start, LANES), LANES)

    def forward_chunk(c, carry):
        def tile(i, carry):
            inner = lanes(i * LANES)
            start = c * WIDE + i * LANES
            cols = lanes(start)
            filtered = []
            for n, (x, out) in enumerate(((q_ref, qf_ref), (k_ref, kf_ref), (v_ref, vf_ref))):
                ext[n, :HALO, :] = tail_in[n, :, cols].astype(F32)[EDGE - HALO :]
                ext[n, HALO : HALO + length, :] = x[:, cols].astype(F32)
                weight = w_ref[:, lanes(n * channels + start)]
                total = weight[0:1] * ext[n, HALO : HALO + length, :]
                for j in range(1, fir_len):
                    total = total + weight[j : j + 1] * (ext[n, HALO - j : HALO - j + length, :] * back_masks[j])
                out[:, cols] = total
                filtered.append(total)
            query, key, value = filtered
            mixed = (key * value).astype(BF16)
            mixed_ref[:, cols] = mixed
            mixed_out[c, :, inner] = (mixed.astype(F32) * back_masks[fir_len]).astype(BF16)
            grad = (og_ref[:, cols].astype(F32) * query).astype(BF16)
            grad_ref[:, cols] = grad
            grad_out[c, :, inner] = (grad.astype(F32) * back_masks[fir_len + 1]).astype(BF16)
            return carry

        lax.fori_loop(0, tiles, tile, 0)
        pl.when(has_after)(lambda: mixed_copy(c).start())
        pl.when(has_before)(lambda: grad_copy(c).start())
        return carry

    lax.fori_loop(0, chunks, forward_chunk, 0)

    def long_tile(c, i, u):
        inner = lanes(i * LANES)
        start = c * WIDE + i * LANES
        cols = lanes(start)
        rows = pl.ds(pl.multiple_of((c * tiles + i) * per_tile, per_tile), per_tile)
        taps = taps_ref[rows, :]
        turned = turned_ref[rows, :]
        grad = grad_ref[:, cols]
        both = jnp.concatenate([mixed_ref[:, cols], mixed_in[c, :, inner]], axis=0)
        both_grad = jnp.concatenate([grad, grad_in[c, :, inner]], axis=0)
        flipped = jnp.dot(back[...], grad, preferred_element_type=F32)
        for g in range(per_tile):
            here = slice(g * length, (g + 1) * length)
            ring = pltpu.roll(
                jnp.broadcast_to(turned[g : g + 1], (length, length)), 0, 1, stride=1, stride_axis=0
            ).astype(BF16)
            left[u, here, :length] = ring * masks[0]
            left[u, here, length:] = ring * masks[1]
            ring_t = pltpu.roll(
                jnp.broadcast_to(taps[g : g + 1], (length, length)), 0, 1, stride=1, stride_axis=0
            ).astype(BF16)
            left_t[u, here, :length] = ring_t * masks[2]
            left_t[u, here, length:] = ring_t * masks[3]
            left_p[u, here, :] = jnp.where(group_of_lane == g, flipped, 0.0).astype(BF16)
        prod[u] = jnp.dot(left[u], both, preferred_element_type=F32)
        prod_t[u] = jnp.dot(left_t[u], both_grad, preferred_element_type=F32)
        prod_p[u] = lax.dot_general(left_p[u], both, (((1,), (1,)), ((), ())), preferred_element_type=F32)
        conv = prod[u, :length, :]
        mixed_grad = prod_t[u, :length, :]
        sums = []
        for g in range(per_tile):
            here = slice(g * length, (g + 1) * length)
            if g:
                conv = jnp.where(group_of_lane == g, prod[u, here, :], conv)
                mixed_grad = jnp.where(group_of_lane == g, prod_t[u, here, :], mixed_grad)
            pair = prod_p[u, here, :length] * rev_masks[0] + prod_p[u, here, length:] * rev_masks[1]
            pair = pltpu.roll(pair, 0, 1, stride=1, stride_axis=0)
            sums.append(jnp.sum(pair, axis=0, keepdims=True))
        part[c * slices + i // PAIR, 3 * HALO :, u * LANES : (u + 1) * LANES] = jnp.concatenate(sums, axis=0)
        gated_ref[:, cols] = (qf_ref[:, cols] * conv).astype(BF16)
        products = (
            og_ref[:, cols].astype(F32) * conv, mixed_grad * vf_ref[:, cols], mixed_grad * kf_ref[:, cols],
        )
        for n, product in enumerate(products):
            rounded = product.astype(BF16)
            short_ref[n, :, cols] = rounded
            edge = rounded[:EDGE].astype(F32) * back_masks[fir_len + 1, :EDGE, :]
            head_out[c, n, :, inner] = edge.astype(BF16)

    def long_chunk(c, carry):
        pl.when(has_before)(lambda: mixed_copy(c).wait_recv())
        pl.when(has_after)(lambda: grad_copy(c).wait_recv())

        def pair(i, carry):
            for u in range(PAIR):
                long_tile(c, i * PAIR + u, u)
            return carry

        lax.fori_loop(0, tiles // PAIR, pair, 0)
        pl.when(has_before)(lambda: head_copy(c).start())
        return carry

    lax.fori_loop(0, chunks, long_chunk, 0)

    def part_copy(target, source):
        return copy(part.at[target], slots.at[source], part_send.at[target], part_recv.at[source], target)

    def backward_chunk(c, carry):
        pl.when(has_after)(lambda: head_copy(c).wait_recv())

        def pair(i, carry):
            for u in range(PAIR):
                inner = lanes((i * PAIR + u) * LANES)
                start = c * WIDE + (i * PAIR + u) * LANES
                cols = lanes(start)
                for n, (x, out) in enumerate(((q_ref, gq_ref), (k_ref, gk_ref), (v_ref, gv_ref))):
                    e = u * 3 + n
                    ext[e, :length, :] = short_ref[n, :, cols].astype(F32)
                    ext[e, length : length + HALO, :] = head_in[c, n, :, inner].astype(F32)[:HALO]
                    weight = w_ref[:, lanes(n * channels + start)]
                    signal = x[:, cols].astype(F32)
                    total = None
                    sums = []
                    for j in range(fir_len):
                        moved = ext[e, j : j + length, :]
                        if j:
                            moved = moved * fore_masks[j]
                        term = weight[j : j + 1] * moved
                        total = term if total is None else total + term
                        sums.append(jnp.sum(signal * moved, axis=0, keepdims=True))
                    sums.append(jnp.zeros((HALO - fir_len, LANES), F32))
                    out[:, cols] = total.astype(BF16)
                    part[c * slices + i, n * HALO : (n + 1) * HALO, u * LANES : (u + 1) * LANES] = jnp.concatenate(
                        sums, axis=0
                    )
            return carry

        lax.fori_loop(0, slices, pair, 0)
        if summed:
            for s in range(slices):
                target = c * slices + s

                @pl.when(target != me)
                def _():
                    part_copy(target, me).start()

        return carry

    lax.fori_loop(0, chunks, backward_chunk, 0)

    if summed:
        def add(d, total):
            source = lax.rem(me + d, count)
            part_copy(me, source).wait_recv()
            return total + slots[source]

        total = lax.fori_loop(1, count, add, part[me])
        kind = lax.broadcasted_iota(jnp.int32, total.shape, 0)
        sums_ref[me] = total * jnp.where(kind < 3 * HALO, short_scale, med_scale)
        core = lax.rem(me, 2)
        other = me + 1 - 2 * core

        def sum_copy(slot, way, peer):
            return copy(sums_ref.at[slot], sums_ref.at[slot], sum_send.at[way], sum_recv.at[slot], peer)

        chips = count // 2
        for d in range(1, chips):
            sum_copy(me, d, lax.rem(me + 2 * d, count)).start()
        sum_copy(me, 0, other).start()
        for d in range(1, chips):
            slot = lax.rem(me + count - 2 * d, count)
            sum_copy(slot, d, other).wait_recv()
            sum_copy(slot, chips + d, other).start()
        for d in range(chips):
            slot = lax.rem(other + count - 2 * d, count)
            sum_copy(slot, d, other).wait_recv()
        for d in range(1, chips):
            sum_copy(me, d, lax.rem(me + 2 * d, count)).wait_send()
            sum_copy(me, chips + d, other).wait_send()
        sum_copy(me, 0, other).wait_send()

        def drain(d, carry):
            part_copy(lax.rem(me + d, count), me).wait_send()
            return carry

        lax.fori_loop(1, count, drain, 0)
    else:
        sums_ref[...] = part[...]

    @pl.when(has_after)
    def _():
        tail_copy().wait_send()

    def finish(c, carry):
        @pl.when(has_after)
        def _():
            mixed_copy(c).wait_send()

        @pl.when(has_before)
        def _():
            grad_copy(c).wait_send()
            head_copy(c).wait_send()

        return carry

    lax.fori_loop(0, chunks, finish, 0)


def local(query_proj, key_proj, value_proj, out_grad, short_taps, medium_taps, doc_starts, continues):
    length, channels = query_proj.shape
    groups, med_len = medium_taps.shape
    size = channels // groups
    per_tile = LANES // size
    fir_len = short_taps.shape[0]
    count = lax.axis_size("ctx")
    chunks, pieces = channels // WIDE, channels // SLICE
    summed = pieces == count
    tokens = length * count
    short_scale = 1.0 / math.sqrt(tokens)
    med_scale = 1.0 / math.sqrt(tokens * size)
    taps_f = short_taps.astype(F32)
    med_f = medium_taps.astype(F32)
    turned = jnp.roll(jnp.flip(med_f, axis=1), 1, axis=1)
    shape = jax.ShapeDtypeStruct
    half = shape((length, channels), BF16)
    vmem = pl.BlockSpec(memory_space=pltpu.VMEM)
    smem = pl.BlockSpec(memory_space=pltpu.SMEM)
    dma = pltpu.SemaphoreType.DMA
    buffer = pltpu.VMEM
    gated, gq, gk, gv, sums = pl.pallas_call(
        functools.partial(layer, count, summed, short_scale, med_scale),
        in_specs=[smem] * 2 + [vmem] * 7,
        out_specs=[vmem] * 5,
        out_shape=[half] * 4 + [shape((pieces, 4 * HALO, SLICE), F32)],
        scratch_shapes=[buffer((length, channels), F32)] * 3
        + [buffer((length, channels), BF16)] * 2
        + [buffer((3, length, channels), BF16)]
        + [buffer((3, EDGE, channels), BF16)] * 2
        + [buffer((chunks, length, WIDE), BF16)] * 4
        + [buffer((chunks, 3, EDGE, WIDE), BF16)] * 2
        + [buffer((pieces, 4 * HALO, SLICE), F32)] * 2
        + [
            buffer((fir_len + 2, length, LANES), F32),
            buffer((fir_len, length, LANES), F32),
            buffer((4, length, length), BF16),
            buffer((2, length, length), F32),
            buffer((length, length), BF16),
            buffer((3 * PAIR, length + HALO, LANES), F32),
            buffer((PAIR, per_tile * length, 2 * length), BF16),
            buffer((PAIR, per_tile * length, 2 * length), BF16),
            buffer((PAIR, per_tile * length, LANES), BF16),
            buffer((PAIR, per_tile * length, LANES), F32),
            buffer((PAIR, per_tile * length, LANES), F32),
            buffer((PAIR, per_tile * length, 2 * length), F32),
        ]
        + [dma(())] * 2
        + [dma((chunks,))] * 6
        + [dma((count,))] * 4,
        compiler_params=pltpu.CompilerParams(
            vmem_limit_bytes=VMEM_BYTES, collective_id=0, has_side_effects=True
        ),
    )(doc_starts, continues, query_proj, key_proj, value_proj, out_grad, taps_f, med_f, turned)
    if not summed:
        sums = lax.psum(sums, "ctx")
        sums = jnp.concatenate([sums[:, : 3 * HALO] * short_scale, sums[:, 3 * HALO :] * med_scale], axis=1)
    short = sums[:, : 3 * HALO].reshape(pieces, 3, HALO, SLICE)[:, :, :fir_len]
    grad_short = short.transpose(2, 1, 0, 3).reshape(fir_len, 3 * channels)
    medium = sums[:, 3 * HALO :].reshape(pieces, HALO, SLICE // LANES, LANES).transpose(0, 2, 1, 3)
    grad_medium = jnp.flip(medium.reshape(groups, med_len), axis=1)
    return gated, gq, gk, gv, grad_short, grad_medium


def solution(mesh):
    tokens = P(("grp", "ctx"), None)
    in_specs = (tokens,) * 4 + (P(), P(), tokens, P(("grp", "ctx")))
    out_specs = (tokens,) * 4 + (P("grp", None), P("grp", None))
    return jax.shard_map(local, mesh=mesh, in_specs=in_specs, out_specs=out_specs, check_vma=False)
```

time: 424 us -> 85.5 us (0.20)
  local copies, waits for them, and re-layouts: 129 us -> 10.4 us
  matrix products: 96 us -> 0 us
  other arithmetic: 88.2 us -> 0.14 us
  waiting for transfers between devices: 79.1 us -> 0 us
  Pallas kernels: 0 us -> 73.1 us
  between operations: 15.3 us -> 1.39 us
  starting transfers between devices: 13.1 us -> 0 us
    dot_general x13 -> x0, matrix products: 96 us -> none  [the longest x8 42.1 us: add_diagonals(): jnp.einsum('tgc,egc->gte', grad_rows, window_rows, preferred_element_type...]
    psum x1 -> x0, waiting for transfers between devices: 78.2 us -> none  [local(): short_sum, long_sum = lax.psum((jnp.stack(short_local), long_local), 'ctx')]
    pallas_call x0 -> x1, Pallas kernels: none -> 73.1 us  [local(): pl.pallas_call(functools.partial(layer, count, summed, short_scale, med_s...]
    convert_element_type x4 -> x0, local copies, waits for them, and re-layouts: 38.9 us -> none  [the longest x1 25.8 us: local(): toeplitz = jnp.einsum('gl,lte->gte', medium_taps, lag_table, preferred_el...]
    while x9 -> x0, local copies, waits for them, and re-layouts: 29 us -> none
    slice x10 -> x4, local copies, waits for them, and re-layouts: 28.3 us -> 1.19 us  [the longest x3 1.18 us: local(): turned = jnp.roll(jnp.flip(med_f, axis=1), 1, axis=1)]
    reduce_sum x10 -> x0, other arithmetic: 26.6 us -> none  [the longest x8 13.9 us: add_diagonals(): return totals + jnp.sum(banded_stripes, axis=1)]
    add x11 -> x0, other arithmetic: 19.2 us -> none  [the longest x8 11.8 us: add_diagonals(): return totals + jnp.sum(banded_stripes, axis=1)]
  transfers between devices with their start and end apart: 5 -> 0, of which waited for: 2 -> 0; matrix products, arithmetic and copies ran while one was open for 32% -> 0% of each run, Pallas kernels for 0% -> 0%
where the time goes in v2:
time: 85.5 us; the launch traced here: 85 us
  Pallas kernels  73.1 us (85%)
  local copies, waits for them, and re-layouts  10.4 us (12%)
  between operations  1.39 us (2%)
    pallas_call x1, Pallas kernels, local(): pl.pallas_call(functools.partial(layer, count, summed, short_scale, med_s...  73.1 us
    unnamed x19, local copies, waits for them, and re-layouts  8.17 us

profile of v2, /device:TPU:1, one launch (start us, length us, event | category | flops | bytes accessed | tf_op | source)
XLA Modules:
  0.0 85.0 jit_solution(1373753030271628906)
XLA Ops:
  1.3 0.0 copy-start.1
  1.3 0.9 %slice.27 = f32[256,1]{1,0:T(8,128)S(1)} slice(bf16[256,128]{1,0:T(8,128)(2,1)} %param.13), slice={[0:256], [0:1]} | slice | bytes 2048 | tf_op jit(solution)/shard_map/jit(_roll_static)/slice | solution.py:350
  2.2 0.0 copy-done.1
  2.2 0.1 slice.28
  2.3 0.2 slice.23
  2.5 0.0 copy-start.6
  2.5 0.1 pad_maximum_fusion.turned_ref
  2.6 0.8 copy-done.6
  3.4 0.0 copy-start
  3.5 0.6 copy-done
  4.1 73.1 %shard_map.127 = (bf16[128,4096]{1,0:T(8,128)(2,1)}, bf16[128,4096]{1,0:T(8,128)(2,1)}, bf16[128,4096]{1,0:T(8,128)(2,1)}, bf16[128,4096]{1,0:T(8,128)(2,1)}, f32[16,32,256]{2,1,0:T(8,128)S(1)}) custom-call(s32[1,2]{1,0:T(1,128)S(1)} %copy-done, s32[1]{0:T(128)S(6)} %copy.20.flag, bf16[128,4096]{1,0:T(8,128)(2,1)} %q_ref.1, bf16[128,4096]{1,0:T(8,128)(2,1)} %k_ref.1, ...), custom_call_target="tpu_custom_call" | custom-call | tf_op jit(solution)/shard_map/pallas_call | solution.py:357
  77.3 0.0 copy-start.5
  77.3 0.1 copy.14
  77.5 0.8 rev.5
  78.3 1.0 %copy.15 = f32[1,7,48,256]{3,1,2,0:T(8,128)} copy(f32[1,7,48,256]{3,2,1,0:T(8,128)S(1)} %bitcast.12) | data formatting | bytes 688128
  79.2 0.0 copy-done.5
  79.2 0.0 copy-start.4
  79.2 1.0 %copy.21 = bf16[128,4096]{1,0:T(8,128)(2,1)} copy(bf16[128,4096]{1,0:T(8,128)(2,1)S(1)} %copy-done.5) | data formatting | bytes 2097152
  80.2 0.6 copy-done.4
  80.8 0.0 copy-start.3
  80.8 1.0 %copy.22 = bf16[128,4096]{1,0:T(8,128)(2,1)} copy(bf16[128,4096]{1,0:T(8,128)(2,1)S(1)} %copy-done.4) | data formatting | bytes 2097152
  81.8 0.6 copy-done.3
  82.5 0.0 copy-start.2
  82.5 1.0 %copy.23 = bf16[128,4096]{1,0:T(8,128)(2,1)} copy(bf16[128,4096]{1,0:T(8,128)(2,1)S(1)} %copy-done.3) | data formatting | bytes 2097152
  83.4 0.6 copy-done.2
  84.1 1.0 %copy.24 = bf16[128,4096]{1,0:T(8,128)(2,1)} copy(bf16[128,4096]{1,0:T(8,128)(2,1)S(1)} %copy-done.2) | data formatting | bytes 2097152
  (5 shorter events, 0.1 us)
Async XLA Ops:
  1.3 0.9 %copy-start.1 = (bf16[256,128]{1,0:T(8,128)(2,1)S(1)}, bf16[256,128]{1,0:T(8,128)(2,1)}, u32[]{:S(2)}) copy-start(bf16[256,128]{1,0:T(8,128)(2,1)} %param.13) | copy-start | bytes 196612
  2.5 0.9 %copy-start.6 = (bf16[7,12288]{1,0:T(8,128)(2,1)S(1)}, bf16[7,12288]{1,0:T(8,128)(2,1)}, u32[]{:S(2)}) copy-start(bf16[7,12288]{1,0:T(8,128)(2,1)} %param.12) | copy-start | bytes 516100
  3.4 0.7 copy-start
  77.3 1.9 %copy-start.5 = (bf16[128,4096]{1,0:T(8,128)(2,1)S(1)}, bf16[128,4096]{1,0:T(8,128)(2,1)}, u32[]{:S(2)}) copy-start(bf16[128,4096]{1,0:T(8,128)(2,1)} %get-tuple-element.22) | copy-start | bytes 3145732
  79.2 1.6 %copy-start.4 = (bf16[128,4096]{1,0:T(8,128)(2,1)S(1)}, bf16[128,4096]{1,0:T(8,128)(2,1)}, u32[]{:S(2)}) copy-start(bf16[128,4096]{1,0:T(8,128)(2,1)} %get-tuple-element.23) | copy-start | bytes 3145732
  80.8 1.6 %copy-start.3 = (bf16[128,4096]{1,0:T(8,128)(2,1)S(1)}, bf16[128,4096]{1,0:T(8,128)(2,1)}, u32[]{:S(2)}) copy-start(bf16[128,4096]{1,0:T(8,128)(2,1)} %get-tuple-element.24) | copy-start | bytes 3145732
  82.5 1.6 %copy-start.2 = (bf16[128,4096]{1,0:T(8,128)(2,1)S(1)}, bf16[128,4096]{1,0:T(8,128)(2,1)}, u32[]{:S(2)}) copy-start(bf16[128,4096]{1,0:T(8,128)(2,1)} %get-tuple-element.25) | copy-start | bytes 3145732

commit v3 on v2

--- a/solution.py
+++ b/solution.py
@@ -31,12 +31,12 @@
 def layer(
     count, summed, short_scale, med_scale,
     starts, flag, q_ref, k_ref, v_ref, og_ref, w_ref, taps_ref, turned_ref,
-    gated_ref, gq_ref, gk_ref, gv_ref, sums_ref,
-    qf_ref, kf_ref, vf_ref, mixed_ref, grad_ref, short_ref,
+    gated_out, gq_out, gk_out, gv_out, sums_ref,
+    gated_ref, gq_ref, gk_ref, gv_ref, qf_ref, kf_ref, vf_ref, mixed_ref, grad_ref, short_ref,
     tail_out, tail_in, mixed_out, mixed_in, grad_out, grad_in, head_out, head_in, part, slots,
     back_masks, fore_masks, masks, rev_masks, back, ext, left, left_t, left_p, prod, prod_t, prod_p,
     tail_send, tail_recv, mixed_send, mixed_recv, grad_send, grad_recv, head_send, head_recv,
-    part_send, part_recv, sum_send, sum_recv,
+    part_send, part_recv, sum_send, sum_recv, store_sem,
 ):
     length, channels = q_ref.shape
     fir_len = w_ref.shape[0]
@@ -228,11 +228,19 @@
         return carry
 
     lax.fori_loop(0, chunks, long_chunk, 0)
+    stores = [
+        pltpu.make_async_copy(src, dst, store_sem.at[n])
+        for n, (src, dst) in enumerate(
+            ((gated_ref, gated_out), (gq_ref, gq_out), (gk_ref, gk_out), (gv_ref, gv_out))
+        )
+    ]
+    stores[0].start()
 
     def part_copy(target, source):
         return copy(part.at[target], slots.at[source], part_send.at[target], part_recv.at[source], target)
 
-    def backward_chunk(c, carry):
+    def backward_chunk(step, carry):
+        c = lax.rem(step + 1 + me // slices, chunks)
         pl.when(has_after)(lambda: head_copy(c).wait_recv())
 
         def pair(i, carry):
@@ -274,6 +282,8 @@
         return carry
 
     lax.fori_loop(0, chunks, backward_chunk, 0)
+    for store in stores[1:]:
+        store.start()
 
     if summed:
         def add(d, total):
@@ -331,6 +341,8 @@
         return carry
 
     lax.fori_loop(0, chunks, finish, 0)
+    for store in stores:
+        store.wait()
 
 
 def local(query_proj, key_proj, value_proj, out_grad, short_taps, medium_taps, doc_starts, continues):
@@ -357,9 +369,10 @@
     gated, gq, gk, gv, sums = pl.pallas_call(
         functools.partial(layer, count, summed, short_scale, med_scale),
         in_specs=[smem] * 2 + [vmem] * 7,
-        out_specs=[vmem] * 5,
+        out_specs=[pl.BlockSpec(memory_space=pl.ANY)] * 4 + [vmem],
         out_shape=[half] * 4 + [shape((pieces, 4 * HALO, SLICE), F32)],
-        scratch_shapes=[buffer((length, channels), F32)] * 3
+        scratch_shapes=[buffer((length, channels), BF16)] * 4
+        + [buffer((length, channels), F32)] * 3
         + [buffer((length, channels), BF16)] * 2
         + [buffer((3, length, channels), BF16)]
         + [buffer((3, EDGE, channels), BF16)] * 2
@@ -382,7 +395,8 @@
         ]
         + [dma(())] * 2
         + [dma((chunks,))] * 6
-        + [dma((count,))] * 4,
+        + [dma((count,))] * 4
+        + [dma((4,))],
         compiler_params=pltpu.CompilerParams(
             vmem_limit_bytes=VMEM_BYTES, collective_id=0, has_side_effects=True
         ),

time: 85.5 us -> 84.9 us (level)
  no operation moved by 1% of the time
where the time goes in v3:
time: 84.9 us; the launch traced here: 84.5 us
  Pallas kernels  72.6 us (86%)
  local copies, waits for them, and re-layouts  10.4 us (12%)
  between operations  1.39 us (2%)
    pallas_call x1, Pallas kernels, local(): pl.pallas_call(functools.partial(layer, count, summed, short_scale, med_s...  72.6 us
    unnamed x19, local copies, waits for them, and re-layouts  8.17 us

profile of v3, /device:TPU:1, one launch (start us, length us, event | category | flops | bytes accessed | tf_op | source)
XLA Modules:
  0.0 84.5 jit_solution(10940875822728080502)
XLA Ops:
  1.3 0.0 copy-start.1
  1.3 0.9 %slice.27 = f32[256,1]{1,0:T(8,128)S(1)} slice(bf16[256,128]{1,0:T(8,128)(2,1)} %param.13), slice={[0:256], [0:1]} | slice | bytes 2048 | tf_op jit(solution)/shard_map/jit(_roll_static)/slice | solution.py:362
  2.2 0.0 copy-done.1
  2.2 0.1 slice.28
  2.3 0.2 slice.23
  2.5 0.0 copy-start.6
  2.5 0.1 pad_maximum_fusion.turned_ref
  2.6 0.8 copy-done.6
  3.4 0.0 copy-start
  3.5 0.6 copy-done
  4.1 72.6 %shard_map.127 = (bf16[128,4096]{1,0:T(8,128)(2,1)}, bf16[128,4096]{1,0:T(8,128)(2,1)}, bf16[128,4096]{1,0:T(8,128)(2,1)}, bf16[128,4096]{1,0:T(8,128)(2,1)}, f32[16,32,256]{2,1,0:T(8,128)S(1)}) custom-call(s32[1,2]{1,0:T(1,128)S(1)} %copy-done, s32[1]{0:T(128)S(6)} %copy.20.flag, bf16[128,4096]{1,0:T(8,128)(2,1)} %q_ref.1, bf16[128,4096]{1,0:T(8,128)(2,1)} %k_ref.1, ...), custom_call_target="tpu_custom_call" | custom-call | tf_op jit(solution)/shard_map/pallas_call | solution.py:369
  76.8 0.0 copy-start.5
  76.8 0.1 copy.14
  76.9 0.8 rev.5
  77.8 1.0 %copy.15 = f32[1,7,48,256]{3,1,2,0:T(8,128)} copy(f32[1,7,48,256]{3,2,1,0:T(8,128)S(1)} %bitcast.12) | data formatting | bytes 688128
  78.7 0.0 copy-done.5
  78.7 0.0 copy-start.4
  78.7 1.0 %copy.21 = bf16[128,4096]{1,0:T(8,128)(2,1)} copy(bf16[128,4096]{1,0:T(8,128)(2,1)S(1)} %copy-done.5) | data formatting | bytes 2097152
  79.7 0.6 copy-done.4
  80.3 0.0 copy-start.3
  80.3 1.0 %copy.22 = bf16[128,4096]{1,0:T(8,128)(2,1)} copy(bf16[128,4096]{1,0:T(8,128)(2,1)S(1)} %copy-done.4) | data formatting | bytes 2097152
  81.3 0.6 copy-done.3
  81.9 0.0 copy-start.2
  81.9 1.0 %copy.23 = bf16[128,4096]{1,0:T(8,128)(2,1)} copy(bf16[128,4096]{1,0:T(8,128)(2,1)S(1)} %copy-done.3) | data formatting | bytes 2097152
  82.9 0.6 copy-done.2
  83.5 1.0 %copy.24 = bf16[128,4096]{1,0:T(8,128)(2,1)} copy(bf16[128,4096]{1,0:T(8,128)(2,1)S(1)} %copy-done.2) | data formatting | bytes 2097152
  (5 shorter events, 0.1 us)
Async XLA Ops:
  1.3 0.9 %copy-start.1 = (bf16[256,128]{1,0:T(8,128)(2,1)S(1)}, bf16[256,128]{1,0:T(8,128)(2,1)}, u32[]{:S(2)}) copy-start(bf16[256,128]{1,0:T(8,128)(2,1)} %param.13) | copy-start | bytes 196612
  2.5 0.9 %copy-start.6 = (bf16[7,12288]{1,0:T(8,128)(2,1)S(1)}, bf16[7,12288]{1,0:T(8,128)(2,1)}, u32[]{:S(2)}) copy-start(bf16[7,12288]{1,0:T(8,128)(2,1)} %param.12) | copy-start | bytes 516100
  3.4 0.7 copy-start
  76.8 1.9 %copy-start.5 = (bf16[128,4096]{1,0:T(8,128)(2,1)S(1)}, bf16[128,4096]{1,0:T(8,128)(2,1)}, u32[]{:S(2)}) copy-start(bf16[128,4096]{1,0:T(8,128)(2,1)} %get-tuple-element.22) | copy-start | bytes 3145732
  78.7 1.6 %copy-start.4 = (bf16[128,4096]{1,0:T(8,128)(2,1)S(1)}, bf16[128,4096]{1,0:T(8,128)(2,1)}, u32[]{:S(2)}) copy-start(bf16[128,4096]{1,0:T(8,128)(2,1)} %get-tuple-element.23) | copy-start | bytes 3145732
  80.3 1.6 %copy-start.3 = (bf16[128,4096]{1,0:T(8,128)(2,1)S(1)}, bf16[128,4096]{1,0:T(8,128)(2,1)}, u32[]{:S(2)}) copy-start(bf16[128,4096]{1,0:T(8,128)(2,1)} %get-tuple-element.24) | copy-start | bytes 3145732
  81.9 1.6 %copy-start.2 = (bf16[128,4096]{1,0:T(8,128)(2,1)S(1)}, bf16[128,4096]{1,0:T(8,128)(2,1)}, u32[]{:S(2)}) copy-start(bf16[128,4096]{1,0:T(8,128)(2,1)} %get-tuple-element.25) | copy-start | bytes 3145732

commit v4 on v3

--- a/solution.py
+++ b/solution.py
@@ -135,18 +135,18 @@
         return pl.ds(pl.multiple_of(start, LANES), LANES)
 
     def forward_chunk(c, carry):
-        def tile(i, carry):
+        def tile(i, u):
             inner = lanes(i * LANES)
             start = c * WIDE + i * LANES
             cols = lanes(start)
             filtered = []
             for n, (x, out) in enumerate(((q_ref, qf_ref), (k_ref, kf_ref), (v_ref, vf_ref))):
-                ext[n, :HALO, :] = tail_in[n, :, cols].astype(F32)[EDGE - HALO :]
-                ext[n, HALO : HALO + length, :] = x[:, cols].astype(F32)
+                ext[u * 3 + n, :HALO, :] = tail_in[n, :, cols].astype(F32)[EDGE - HALO :]
+                ext[u * 3 + n, HALO : HALO + length, :] = x[:, cols].astype(F32)
                 weight = w_ref[:, lanes(n * channels + start)]
-                total = weight[0:1] * ext[n, HALO : HALO + length, :]
+                total = weight[0:1] * ext[u * 3 + n, HALO : HALO + length, :]
                 for j in range(1, fir_len):
-                    total = total + weight[j : j + 1] * (ext[n, HALO - j : HALO - j + length, :] * back_masks[j])
+                    total = total + weight[j : j + 1] * (ext[u * 3 + n, HALO - j : HALO - j + length, :] * back_masks[j])
                 out[:, cols] = total
                 filtered.append(total)
             query, key, value = filtered
@@ -156,9 +156,13 @@
             grad = (og_ref[:, cols].astype(F32) * query).astype(BF16)
             grad_ref[:, cols] = grad
             grad_out[c, :, inner] = (grad.astype(F32) * back_masks[fir_len + 1]).astype(BF16)
+
+        def pair(i, carry):
+            for u in range(PAIR):
+                tile(i * PAIR + u, u)
             return carry
 
-        lax.fori_loop(0, tiles, tile, 0)
+        lax.fori_loop(0, tiles // PAIR, pair, 0)
         pl.when(has_after)(lambda: mixed_copy(c).start())
         pl.when(has_before)(lambda: grad_copy(c).start())
         return carry
@@ -345,6 +349,11 @@
         store.wait()
 
 
+def hand_on(*refs):
+    for source, target in zip(refs[:4], refs[4:]):
+        target[...] = source[...]
+
+
 def local(query_proj, key_proj, value_proj, out_grad, short_taps, medium_taps, doc_starts, continues):
     length, channels = query_proj.shape
     groups, med_len = medium_taps.shape
@@ -369,7 +378,7 @@
     gated, gq, gk, gv, sums = pl.pallas_call(
         functools.partial(layer, count, summed, short_scale, med_scale),
         in_specs=[smem] * 2 + [vmem] * 7,
-        out_specs=[pl.BlockSpec(memory_space=pl.ANY)] * 4 + [vmem],
+        out_specs=[pl.BlockSpec(memory_space=pltpu.HBM)] * 4 + [vmem],
         out_shape=[half] * 4 + [shape((pieces, 4 * HALO, SLICE), F32)],
         scratch_shapes=[buffer((length, channels), BF16)] * 4
         + [buffer((length, channels), F32)] * 3
@@ -401,6 +410,15 @@
             vmem_limit_bytes=VMEM_BYTES, collective_id=0, has_side_effects=True
         ),
     )(doc_starts, continues, query_proj, key_proj, value_proj, out_grad, taps_f, med_f, turned)
+    block = pl.BlockSpec((length, channels // 4), lambda i: (0, i))
+    gated, gq, gk, gv = pl.pallas_call(
+        hand_on,
+        grid=(4,),
+        in_specs=[block] * 4,
+        out_specs=[block] * 4,
+        out_shape=[half] * 4,
+        compiler_params=pltpu.CompilerParams(vmem_limit_bytes=VMEM_BYTES),
+    )(gated, gq, gk, gv)
     if not summed:
         sums = lax.psum(sums, "ctx")
         sums = jnp.concatenate([sums[:, : 3 * HALO] * short_scale, sums[:, 3 * HALO :] * med_scale], axis=1)

time: 84.9 us -> 84.7 us (level)
  local copies, waits for them, and re-layouts: 10.4 us -> 5.8 us
  Pallas kernels: 72.6 us -> 77 us
    unnamed x19 -> x9, local copies, waits for them, and re-layouts: 8.17 us -> 3.6 us
    pallas_call x0 -> x1, Pallas kernels: none -> 4.4 us  [local(): pl.pallas_call(hand_on, grid=(4,), in_specs=[block] * 4, out_specs=[block...]
where the time goes in v4:
time: 84.7 us; the launch traced here: 84.3 us
  Pallas kernels  77 us (91%)
  local copies, waits for them, and re-layouts  5.8 us (7%)
  between operations  1.38 us (2%)
    pallas_call x1, Pallas kernels, local(): pl.pallas_call(functools.partial(layer, count, summed, short_scale, med_s...  72.6 us
    pallas_call x1, Pallas kernels, local(): pl.pallas_call(hand_on, grid=(4,), in_specs=[block] * 4, out_specs=[block...  4.4 us
    unnamed x9, local copies, waits for them, and re-layouts  3.6 us

profile of v4, /device:TPU:1, one launch (start us, length us, event | category | flops | bytes accessed | tf_op | source)
XLA Modules:
  0.0 84.3 jit_solution(2148522471126665452)
XLA Ops:
  1.3 0.0 copy-start.2
  1.3 0.9 %slice.27 = f32[256,1]{1,0:T(8,128)S(1)} slice(bf16[256,128]{1,0:T(8,128)(2,1)} %param.13), slice={[0:256], [0:1]} | slice | bytes 2048 | tf_op jit(solution)/shard_map/jit(_roll_static)/slice | solution.py:371
  2.2 0.0 copy-done.2
  2.2 0.1 slice.28
  2.3 0.2 slice.23
  2.5 0.0 copy-start.3
  2.5 0.1 pad_maximum_fusion.turned_ref
  2.6 0.8 copy-done.3
  3.4 0.0 copy-start.1
  3.5 0.6 copy-done.1
  4.1 72.6 %shard_map.127 = (bf16[128,4096]{1,0:T(8,128)(2,1)}, bf16[128,4096]{1,0:T(8,128)(2,1)}, bf16[128,4096]{1,0:T(8,128)(2,1)}, bf16[128,4096]{1,0:T(8,128)(2,1)}, f32[16,32,256]{2,1,0:T(8,128)S(1)}) custom-call(s32[1,2]{1,0:T(1,128)S(1)} %copy-done.1, s32[1]{0:T(128)S(6)} %copy.16.flag, bf16[128,4096]{1,0:T(8,128)(2,1)} %q_ref.1, bf16[128,4096]{1,0:T(8,128)(2,1)} %k_ref.1, ...), custom_call_target="tpu_custom_call" | custom-call | tf_op jit(solution)/shard_map/pallas_call | solution.py:378
  76.7 0.0 copy-start
  76.7 1.2 %copy-done = bf16[128,4096]{1,0:T(8,128)(2,1)S(1)} copy-done((bf16[128,4096]{1,0:T(8,128)(2,1)S(1)}, bf16[128,4096]{1,0:T(8,128)(2,1)}, u32[]{:S(2)}) %copy-start) | copy-done | bytes 1048600
  77.9 4.4 %shard_map.128 = (bf16[128,4096]{1,0:T(8,128)(2,1)}, bf16[128,4096]{1,0:T(8,128)(2,1)}, bf16[128,4096]{1,0:T(8,128)(2,1)}, bf16[128,4096]{1,0:T(8,128)(2,1)}) custom-call(bf16[128,4096]{1,0:T(8,128)(2,1)S(1)} %copy-done, bf16[128,4096]{1,0:T(8,128)(2,1)} %get-tuple-element.16.refs_1_, bf16[128,4096]{1,0:T(8,128)(2,1)} %get-tuple-element.17.refs_2_, ...), custom_call_target="tpu_custom_call" | custom-call | tf_op jit(solution)/shard_map/pallas_call | solution.py:414
  82.4 0.1 copy.14
  82.5 0.8 rev.5
  83.4 1.0 %copy.15 = f32[1,7,48,256]{3,1,2,0:T(8,128)} copy(f32[1,7,48,256]{3,2,1,0:T(8,128)S(1)} %bitcast.12) | data formatting | bytes 688128
  (5 shorter events, 0.1 us)
Async XLA Ops:
  1.3 0.9 %copy-start.2 = (bf16[256,128]{1,0:T(8,128)(2,1)S(1)}, bf16[256,128]{1,0:T(8,128)(2,1)}, u32[]{:S(2)}) copy-start(bf16[256,128]{1,0:T(8,128)(2,1)} %param.13) | copy-start | bytes 196612
  2.5 0.9 %copy-start.3 = (bf16[7,12288]{1,0:T(8,128)(2,1)S(1)}, bf16[7,12288]{1,0:T(8,128)(2,1)}, u32[]{:S(2)}) copy-start(bf16[7,12288]{1,0:T(8,128)(2,1)} %param.12) | copy-start | bytes 516100
  3.4 0.7 copy-start.1
  76.7 1.2 %copy-start = (bf16[128,4096]{1,0:T(8,128)(2,1)S(1)}, bf16[128,4096]{1,0:T(8,128)(2,1)}, u32[]{:S(2)}) copy-start(bf16[128,4096]{1,0:T(8,128)(2,1)} %get-tuple-element.15.refs_0_) | copy-start | bytes 3145732
